TPU v7x, 512 devices: a whole 4x8x8 slice. The times are simulated.
512 devices in a mesh: dp: 64 (over y, z_lo, core), mp: 8 (over x, z_hi).
Axes of the slice: x: 4, y: 8, z: 8 (z_hi: 2, z_lo: 4; z = z_hi * 4 + z_lo), core: 2. Of those that a mesh axis runs over, the one named last changes fastest.
Arguments:
- context: bfloat16 [65536, 4096], P('dp', 'mp'), may hold values from -6 to 6
- w_out: bfloat16 [4096, 4096], P('dp', 'mp'), may hold values from -0.09375 to 0.09375
- residual: bfloat16 [65536, 4096], P('dp', 'mp'), may hold values from -6 to 6
- w_proj: bfloat16 [3584, 4096], P('dp', 'mp'), may hold values from -0.09375 to 0.09375
- hidden: bfloat16 [65536, 3584], P(('dp', 'mp')), may hold values from -6 to 6
- gain: float32 [3584], replicated, may hold values from 0.25 to 1.75
- matched: int32 [24576], P('dp'), may hold values from 0 to 1023, as said below
Outputs:
- grad_hidden: bfloat16 [65536, 3584], P(('dp', 'mp'))
- gain_update: float32 [3584], replicated
Inputs may be any that keep to these rules, and one draw needn't show every extreme that they name: Within a token group the entries are distinct; split a group's 1024 tokens into 8 equal consecutive blocks: each block holds exactly 384 / 8 matched tokens, listed block after block, ascending within a block.
All inputs are finite; a program needn't handle non-finite values.
Results may differ from a plain program's by a relative error of at most 0.018.
Values may be sent and summed in bfloat16 or wider, within the bound.
No kernel may reach another device: no remote copies, remote signals or barrier semaphores. Data moves between devices by JAX's collectives and lax.ppermute only.
A program may use at most 64 MiB of HBM per device.

v0:
```python
import jax
import jax.numpy as jnp
from jax import lax
from jax.sharding import PartitionSpec as P

EPS = 1e-06


def body(context, w_out, residual, w_proj, hidden, gain, matched):
    width = hidden.shape[1]
    own_rows = hidden.shape[0]
    group_size = lax.axis_size("mp")
    position = lax.axis_index("mp")
    pick = matched.shape[0] // group_size
    mine = lax.dynamic_slice_in_dim(matched, position * pick, pick, 0)
    local = mine - position * own_rows
    hid = hidden[local].astype(jnp.float32)
    stat = lax.rsqrt(jnp.mean(hid * hid, axis=-1, keepdims=True) + EPS)
    outgoing = (hid * stat * gain).astype(jnp.bfloat16)
    normed_all = lax.all_gather(outgoing, "mp", axis=0, tiled=True)
    picked_context = context[matched]
    heads = lax.all_gather(picked_context, "mp", axis=1, tiled=True)
    out_all, proj_all = (
        lax.all_gather(w_out, "dp", axis=0, tiled=True),
        lax.all_gather(w_proj, "dp", axis=0, tiled=True),
    )
    attended = jnp.dot(heads, out_all, preferred_element_type=jnp.float32)
    teacher = residual[matched].astype(jnp.float32) + attended
    pred = jnp.dot(normed_all, proj_all, preferred_element_type=jnp.float32)
    g_pred = (pred - teacher).astype(jnp.bfloat16)
    term = lax.dot_general(
        g_pred, proj_all, (((1,), (1,)), ((), ())), preferred_element_type=jnp.float32
    )
    g_normed = lax.psum_scatter(
        term.astype(jnp.bfloat16), "mp", scatter_dimension=0, tiled=True
    ).astype(jnp.float32)
    scaled = g_normed * gain
    inner = jnp.sum(hid * scaled, axis=-1, keepdims=True)
    grad_rows = (stat * scaled - hid * stat * stat * stat * inner / width).astype(jnp.bfloat16)
    grad_hidden = jnp.zeros((own_rows, width), jnp.bfloat16).at[local].set(grad_rows)
    local_gain = jnp.sum(g_normed * hid * stat, axis=0)
    grad_gain = lax.psum(local_gain, ("dp", "mp"))
    gain_update = grad_gain * lax.rsqrt(jnp.mean(grad_gain * grad_gain) + EPS)
    return (grad_hidden, gain_update)


def solution(mesh):
    return jax.shard_map(
        body,
        mesh=mesh,
        in_specs=(
            P("dp", "mp"),
            P("dp", "mp"),
            P("dp", "mp"),
            P("dp", "mp"),
            P(("dp", "mp"), None),
            P(),
            P("dp"),
        ),
        out_specs=(P(("dp", "mp"), None), P()),
        check_vma=False,
    )
```

profile of v0, /device:TPU:1, one launch (start us, length us, event | category | flops | bytes accessed | tf_op | source)
XLA Modules:
  0.0 673.4 jit_solution(13954791330464753049)
XLA Ops:
  7.2 0.0 copy-start
  7.2 0.0 copy-start.3
  7.2 0.0 all-gather.6.cloned.1.call-start
  7.2 0.8 compare_select_fusion.1
  8.1 0.0 copy-start.1
  8.1 2.5 gather_fusion
  10.6 0.2 fusion.11
  10.8 1.6 fusion.5
  12.4 0.0 all-gather.6.cloned.1.call-update
  12.4 0.0 all-gather.8.cloned.1.call-start
  12.4 0.7 all-gather.8.cloned.1.call-update
  13.1 0.0 all-gather.12.cloned.1.call-start
  13.2 0.0 copy-done.3
  13.2 0.0 copy-done
  13.2 2.6 gather_fusion.2
  15.8 0.0 all-gather.12.cloned.1.call-update
  15.8 0.0 all-gather.10.cloned.1.call-start
  15.9 0.5 all-gather.10.cloned.1.call-update
  16.4 0.0 reduce-scatter.2.cloned.1.call-start
  16.5 0.0 copy-done.1
  16.5 2.1 gather_fusion.1
  18.5 90.5 %all-gather.6.cloned.1.call-done = bf16[384,3584]{1,0:T(8,128)(2,1)} async-done(((bf16[48,3584]{1,0:T(8,128)(2,1)}), bf16[384,3584]{1,0:T(8,128)(2,1)}) %all-gather.6.cloned.1.call-update) | async-done | bytes 2752528 | tf_op jit(solution)/shard_map/all_gather | solution.py:20
  109.1 119.1 %all-gather.8.cloned.1.call-done = bf16[3584,512]{1,0:T(8,128)(2,1)} async-done(((bf16[56,512]{1,0:T(8,128)(2,1)}), bf16[3584,512]{1,0:T(8,128)(2,1)}) %all-gather.8.cloned.1.call-update) | async-done | bytes 3670032 | tf_op jit(solution)/shard_map/all_gather | solution.py:25
  228.1 4.4 fusion.22
  232.6 0.0 copy-start.2
  232.6 95.5 %all-gather.12.cloned.1.call-done = bf16[384,4096]{1,0:T(8,128)(2,1)} async-done(((bf16[384,512]{1,0:T(8,128)(2,1)}), bf16[384,4096]{1,0:T(8,128)(2,1)}) %all-gather.12.cloned.1.call-update) | async-done | bytes 3145744 | tf_op jit(solution)/shard_map/all_gather | solution.py:22
  328.1 120.1 %all-gather.10.cloned.1.call-done = bf16[4096,512]{1,0:T(8,128)(2,1)} async-done(((bf16[64,512]{1,0:T(8,128)(2,1)}), bf16[4096,512]{1,0:T(8,128)(2,1)}) %all-gather.10.cloned.1.call-update) | async-done | bytes 4194320 | tf_op jit(solution)/shard_map/all_gather | solution.py:24
  448.2 9.1 %convolution_convert_fusion = bf16[384,3584]{1,0:T(8,128)(2,1)} fusion(bf16[3584,512]{1,0:T(8,128)(2,1)} %all-gather.8.cloned.1.call-done, f32[384,512]{1,0:T(8,128)S(1)} %fusion.22, bf16[384,4096]{1,0:T(8,128)(2,1)} %all-gather.12.cloned.1.call-done, bf16[4096,512]{1,0:T(8,128)(2,1)} %all-gather.10.cloned.1.call-done, bf16[384,512]{1,0:T(8,128)(2,1)S(1)} %gather_fusion.1), kind=kOutput, calls=%fused_computation.4 | convolution fusion | flops 3022061568 | bytes 14942208 | tf_op jit(solution)/shard_map/dot_general | solution.py:31
  457.3 0.0 reduce-scatter.2.cloned.1.call-update
  457.3 106.2 %reduce-scatter.2.cloned.1.call-done = bf16[48,3584]{1,0:T(8,128)(2,1)} async-done(((bf16[384,3584]{1,0:T(8,128)(2,1)}), bf16[48,3584]{1,0:T(8,128)(2,1)}) %reduce-scatter.2.cloned.1.call-update) | async-done | bytes 344080 | tf_op jit(solution)/shard_map/reduce_scatter | solution.py:34
  563.5 0.0 copy-done.2
  563.5 1.3 fusion.14
  564.8 97.4 %psum.7 = f32[3584]{0:T(1024)S(1)} all-reduce(f32[3584]{0:T(1024)S(1)} %get-tuple-element.2), channel_id=1, replica_groups=mesh['dp'=64,'mp'=8] {'dp','mp'}, use_global_device_ids=true, to_apply=%region_5.0 | all-reduce | flops 3584 | bytes 28672 | tf_op jit(solution)/shard_map/psum | solution.py:42
  662.2 0.6 multiply_reduce_fusion
  663.5 0.6 broadcast_multiply_fusion
  664.1 2.8 scatter_custom_fusion
  (4 shorter events, 0.0 us)
Async XLA Ops:
  7.2 6.1 copy-start
  7.2 6.0 copy-start.3
  7.2 101.9 %all-gather.6.cloned.1.call-start = ((), (), s32[]{:S(2)}) async-start(), calls=%async_computation.1 | async-start | bytes 3096576 | tf_op jit(solution)/shard_map/all_gather | solution.py:20
  8.1 8.4 %copy-start.1 = (bf16[1024,512]{1,0:T(8,128)(2,1)S(1)}, bf16[1024,512]{1,0:T(8,128)(2,1)}, u32[]{:S(2)}) copy-start(bf16[1024,512]{1,0:T(8,128)(2,1)} %param.9) | copy-start | bytes 3145732
  12.4 215.7 %all-gather.8.cloned.1.call-start = ((), (), s32[]{:S(2)}) async-start(), calls=%async_computation.2 | async-start | bytes 3727360 | tf_op jit(solution)/shard_map/all_gather | solution.py:25
  13.1 315.0 %all-gather.12.cloned.1.call-start = ((), (), s32[]{:S(2)}) async-start(), calls=%async_computation.5 | async-start | bytes 3538944 | tf_op jit(solution)/shard_map/all_gather | solution.py:22
  15.8 432.3 %all-gather.10.cloned.1.call-start = ((), (), s32[]{:S(2)}) async-start(), calls=%async_computation.3 | async-start | bytes 4259840 | tf_op jit(solution)/shard_map/all_gather | solution.py:24
  16.4 547.1 %reduce-scatter.2.cloned.1.call-start = ((), (), s32[]{:S(2)}) async-start(), calls=%async_computation.4 | async-start | bytes 3096576 | tf_op jit(solution)/shard_map/reduce_scatter | solution.py:34
  232.6 330.9 %copy-start.2 = (f32[3584]{0:T(1024)S(1)}, f32[3584]{0:T(1024)}, u32[]{:S(2)}) copy-start(f32[3584]{0:T(1024)} %param.12) | copy-start | bytes 43012
Sparse Core Ops, SparseCore 0:
  12.5 96.5 all-gather.5
  111.2 116.8 all-gather.7
  231.8 96.2 all-gather.11
  330.1 118.0 all-gather.9
  457.4 106.0 reduce-scatter.1
where the time goes:
time: 674 us; the launch traced here: 673 us
  waiting for transfers between devices  533 us (79%)
  blocking collectives  97.4 us (14%)
  between operations  14.6 us (2%)
  matrix products  13.6 us (2%)
  other arithmetic  7.93 us (1%)
  local copies, waits for them, and re-layouts  7.15 us (1%)
    all_gather x1, waiting for transfers between devices, body(): lax.all_gather(w_out, 'dp', axis=0, tiled=True)  120 us
    all_gather x1, waiting for transfers between devices, body(): lax.all_gather(w_proj, 'dp', axis=0, tiled=True)  119 us
    reduce_scatter x1, waiting for transfers between devices, body(): lax.psum_scatter(term.astype(jnp.bfloat16), 'mp', scatter_dimension=0, ti...  106 us
    psum x1, blocking collectives, body(): grad_gain = lax.psum(local_gain, ('dp', 'mp'))  97.4 us
    all_gather x1, waiting for transfers between devices, body(): heads = lax.all_gather(picked_context, 'mp', axis=1, tiled=True)  95.5 us
    all_gather x1, waiting for transfers between devices, body(): normed_all = lax.all_gather(outgoing, 'mp', axis=0, tiled=True)  90.5 us
  transfers between devices with their start and end apart: 5, of which 5 were waited for; matrix products, arithmetic and copies ran while one was open for 1% of the time, Pallas kernels for 0%

commit v1 on v0

v1 whole, which is shorter than its diff:
```python
import jax
import jax.numpy as jnp
from jax import lax
from jax.experimental import pallas as pl
from jax.experimental.pallas import tpu as pltpu
from jax.sharding import Mesh
from jax.sharding import PartitionSpec as P

EPS = 1e-06
NY, NZL, NC, NX, NZH = 8, 4, 2, 4, 2
NZ = NZL * NZH
AXES = ("y", "zl", "c", "x", "zh")
F32 = jnp.float32
BF16 = jnp.bfloat16


def dev(y, z, c, x):
    return (((y * NZL + z % NZL) * NC + c) * NX + x) * NZH + z // NZL


CHIPS = [(y, z, x) for y in range(NY) for z in range(NZ) for x in range(NX)]


def moved(step):
    pairs = []
    for y, z, x in CHIPS:
        pairs.append((dev(y, z, 0, x), dev((y + step) % NY, z, 0, x)))
        pairs.append((dev(y, z, 1, x), dev(y, (z + step) % NZ, 1, x)))
    return pairs


FORTH, BACK = moved(1), moved(-1)
LINES = [[dev(y, z, 0, x) for z in range(NZ)] for y in range(NY) for x in range(NX)] + [
    [dev(y, z, 1, x) for y in range(NY)] for z in range(NZ) for x in range(NX)
]
FIRST = [
    [dev(h * 4 + y, z, c, x) for c in range(NC) for x in range(NX) for y in range(4)]
    for h in range(2)
    for z in range(NZ)
]
SECOND = [
    [dev(h * 4 + y, z, c, x) for h in range(2) for z in range(NZ)]
    for c in range(NC)
    for x in range(NX)
    for y in range(4)
]


def ring(block):
    held = {0: block}
    ahead = behind = block
    for s in range(1, 4):
        behind = lax.ppermute(behind, AXES, FORTH)
        ahead = lax.ppermute(ahead, AXES, BACK)
        held[8 - s], held[s] = behind, ahead
    half = block.shape[0] // 2
    low = lax.ppermute(behind[:half], AXES, FORTH)
    high = lax.ppermute(ahead[half:], AXES, BACK)
    held[4] = jnp.concatenate([low, high], axis=0)
    return [held[k] for k in range(8)]


def load_all(blocks, wbuf, sems):
    for k, block in enumerate(blocks):
        pltpu.make_async_copy(block, wbuf.at[k], sems.at[k]).start()


def forward_kernel(meta, a_ref, *refs):
    blocks, (out, wbuf, sems) = refs[:8], refs[8:]
    load_all(blocks, wbuf, sems)
    core, z = meta[0], meta[1]
    out[...] = jnp.zeros_like(out)

    def step(k, carry):
        pltpu.make_async_copy(blocks[0], wbuf.at[k], sems.at[k]).wait()

        @pl.when(core == 0)
        def _():
            lanes = pl.ds(pl.multiple_of((k % 2) * 512, 512), 512)
            for g in range(2):
                a = a_ref[g, k // 2, :, lanes]
                for h in range(2):
                    out[g, :, h * 512 : h * 512 + 512] += jnp.dot(
                        a, wbuf[k, h * 512 : h * 512 + 512, :], preferred_element_type=F32
                    )

        @pl.when(core == 1)
        def _():
            zk = (z + k) % NZ
            to = pl.ds(pl.multiple_of((zk // NZL) * 512, 512), 512)
            for g in range(2):
                a = jnp.concatenate(
                    [
                        a_ref[g, x, :, pl.ds(pl.multiple_of(h * 512 + (zk % NZL) * 128, 128), 128)]
                        for x in range(NX)
                        for h in range(NZH)
                    ],
                    axis=1,
                )
                out[g, :, to] += jnp.dot(a, wbuf[k], preferred_element_type=F32)

        return carry

    lax.fori_loop(0, 8, step, 0)


def backward_kernel(a_ref, pred, att, res, *refs):
    blocks, (out, gain_out, g_buf, wbuf, sems) = refs[:8], refs[8:]
    load_all(blocks, wbuf, sems)
    for g in range(2):
        g_buf[g] = (pred[g] - (res[g].astype(F32) + att[1 - g])).astype(BF16)
    nt = (((1,), (1,)), ((), ()))
    for k in range(8):
        pltpu.make_async_copy(blocks[k], wbuf.at[k], sems.at[k]).wait()
        total = jnp.zeros((1, 512), F32)
        for g in range(2):
            term = lax.dot_general(
                g_buf[g, :, :512], wbuf[k, :512, :], nt, preferred_element_type=F32
            ) + lax.dot_general(g_buf[g, :, 512:], wbuf[k, 512:, :], nt, preferred_element_type=F32)
            out[g, :, k * 448 : k * 448 + 448] = term.astype(BF16)[:, :448]
            a = a_ref[g, k // 2, :, (k % 2) * 512 : (k % 2) * 512 + 512].astype(F32)
            total = total + jnp.sum(term * a, axis=0, keepdims=True)
        gain_out[k : k + 1, :] = total


VMEM = pl.BlockSpec(memory_space=pltpu.VMEM)
SMEM = pl.BlockSpec(memory_space=pltpu.SMEM)
ANY = pl.BlockSpec(memory_space=pl.ANY)
PARAMS = pltpu.CompilerParams(vmem_limit_bytes=48 * 1024 * 1024)


def forward(meta, acts, blocks):
    return pl.pallas_call(
        forward_kernel,
        out_shape=jax.ShapeDtypeStruct((2, 192, 1024), F32),
        in_specs=[SMEM, VMEM] + [ANY] * 8,
        out_specs=VMEM,
        scratch_shapes=[pltpu.VMEM((8, 1024, 512), BF16), pltpu.SemaphoreType.DMA((8,))],
        compiler_params=PARAMS,
        cost_estimate=pl.CostEstimate(flops=2 * 384 * 4096 * 1024, bytes_accessed=13 << 20, transcendentals=0),
        name="forward",
    )(meta, acts, *blocks)


def backward(acts, pred, att, res, blocks):
    return pl.pallas_call(
        backward_kernel,
        out_shape=(
            jax.ShapeDtypeStruct((2, 192, 3584), BF16),
            jax.ShapeDtypeStruct((8, 512), F32),
        ),
        in_specs=[VMEM] * 4 + [ANY] * 8,
        out_specs=(VMEM, VMEM),
        scratch_shapes=[
            pltpu.VMEM((2, 192, 1024), BF16),
            pltpu.VMEM((8, 1024, 512), BF16),
            pltpu.SemaphoreType.DMA((8,)),
        ],
        compiler_params=PARAMS,
        cost_estimate=pl.CostEstimate(flops=2 * 384 * 4096 * 1024, bytes_accessed=16 << 20, transcendentals=0),
        name="backward",
    )(acts, pred, att, res, *blocks)


def swapped(pairs):
    return [(dev(y, z, a, x), dev(y, z, b, x)) for y, z, x in CHIPS for a, b in pairs]


def body(context, w_out, residual, w_proj, hidden, gain, matched):
    width = hidden.shape[1]
    own_rows = hidden.shape[0]
    y, c, x, zh = (lax.axis_index(name) for name in ("y", "c", "x", "zh"))
    z = zh * NZL + lax.axis_index("zl")
    first = c == 0

    proj = jnp.pad(w_proj, ((0, 8), (0, 0)))
    got = lax.ppermute(jnp.where(first, w_out, proj), AXES, swapped([(0, 1), (1, 0)]))
    kept = jnp.where(first, proj, w_out)
    pair = jnp.stack([jnp.where(first, kept, got), jnp.where(first, got, kept)])

    blocks = matched.reshape(NX, NZH, 48)
    picks = blocks.transpose(1, 0, 2).reshape(NZH, 192)
    mine = lax.dynamic_index_in_dim(picks, zh, 0, keepdims=False)
    theirs = lax.dynamic_index_in_dim(picks, 1 - zh, 0, keepdims=False)
    away = jnp.concatenate([context[theirs], residual[theirs]], axis=1)
    other = lax.ppermute(away, "zh", [(0, 1), (1, 0)])

    local = lax.dynamic_slice_in_dim(mine, x * 48, 48, 0) - (x * NZH + zh) * own_rows
    hid = hidden[local].astype(F32)
    stat = lax.rsqrt(jnp.mean(hid * hid, axis=-1, keepdims=True) + EPS)
    normed = (hid * stat * gain).astype(BF16).reshape(48, 8, 448)
    normed = jnp.roll(jnp.pad(normed, ((0, 0), (0, 0), (0, 64))), -y, axis=1).reshape(48, 4096)
    normed_all = lax.all_gather(normed, "x", axis=0, tiled=True)

    here = jnp.concatenate([context[mine], residual[mine]], axis=1)
    low = jnp.where(zh == 0, here, other)
    high = jnp.where(zh == 0, other, here)
    heads = jnp.concatenate([low[:, :512], high[:, :512]], axis=1)
    res = jnp.concatenate([low[:, 512:], high[:, 512:]], axis=1)
    heads_all = lax.all_gather(heads, "x", axis=0)
    res_both = jnp.stack([res, lax.ppermute(res, AXES, swapped([(1, 0)]))])

    lines = lax.all_to_all(
        jnp.broadcast_to(pair.reshape(1, 128, 512), (8, 128, 512)), AXES, 0, 0, axis_index_groups=LINES
    )
    tight = jnp.pad(lines.reshape(2, 8, 64, 512)[:, :, :56].reshape(2, 448, 512), ((0, 0), (0, 64), (0, 0)))
    line = jnp.where(first, tight.reshape(1024, 512), lines.reshape(1024, 512))
    held = ring(line)

    normed_all = normed_all.reshape(192, 4, 1024).transpose(1, 0, 2)
    keep = jnp.where(first, normed_all, heads_all)
    give = jnp.where(first, heads_all, normed_all)
    acts = jnp.stack([keep, lax.ppermute(give, AXES, swapped([(0, 1), (1, 0)]))])

    meta = jnp.stack([c, z]).astype(jnp.int32)
    product = forward(meta, acts, held)
    att = lax.ppermute(product, AXES, swapped([(1, 0)]))
    term, gain_rel = backward(acts, product, att, res_both, held)

    term = term.reshape(2, NX, 48, width)
    total = None
    for d in range(1, NX):
        part = lax.dynamic_index_in_dim(term, (x + d) % NX, 1, keepdims=False)
        pairs = [(dev(yy, zz, 0, xx), dev(yy, zz, 0, (xx + d) % NX)) for yy, zz, xx in CHIPS]
        part = lax.ppermute(part, AXES, pairs).astype(F32)
        total = part if total is None else total + part
    total = total + lax.dynamic_index_in_dim(term, x, 1, keepdims=False).astype(F32)
    handed = lax.ppermute(total[1].astype(BF16), AXES, swapped([(0, 1)]))
    g_normed = jnp.where(first, total[0], handed.astype(F32))
    g_normed = jnp.roll(g_normed.reshape(48, 8, 448), y, axis=1).reshape(48, width)

    gain_nat = jnp.roll(gain_rel[:, :448], y, axis=0).reshape(width) / gain
    gain_nat = jnp.where(first, gain_nat, 0.0).reshape(28, 128)
    gathered = lax.all_to_all(
        jnp.broadcast_to(gain_nat[None], (32, 28, 128)), AXES, 0, 0, axis_index_groups=FIRST
    )
    gain_nat = jnp.sum(gathered, axis=0)
    gathered = lax.all_to_all(
        jnp.broadcast_to(gain_nat[None], (16, 28, 128)), AXES, 0, 0, axis_index_groups=SECOND
    )
    grad_gain = jnp.sum(gathered, axis=0).reshape(width)
    gain_update = grad_gain * lax.rsqrt(jnp.mean(grad_gain * grad_gain) + EPS)

    scaled = g_normed * gain
    inner = jnp.sum(hid * scaled, axis=-1, keepdims=True)
    grad_rows = (stat * scaled - hid * stat * stat * stat * inner / width).astype(BF16)
    grad_hidden = jnp.zeros((own_rows, width), BF16).at[local].set(grad_rows)
    return (grad_hidden, gain_update)


def solution(mesh):
    fine = Mesh(mesh.devices.reshape(NY, NZL, NC, NX, NZH), AXES)
    dp, mp = ("y", "zl", "c"), ("x", "zh")
    return jax.shard_map(
        body,
        mesh=fine,
        in_specs=(P(dp, mp), P(dp, mp), P(dp, mp), P(dp, mp), P(dp + mp, None), P(), P(dp)),
        out_specs=(P(dp + mp, None), P()),
        check_vma=False,
    )
```

time: 674 us -> 243 us (0.36)
  waiting for transfers between devices: 533 us -> 54.8 us
  blocking collectives: 97.4 us -> 0 us
  starting transfers between devices: 0.2 us -> 93.1 us
  local copies, waits for them, and re-layouts: 7.15 us -> 30.2 us
  Pallas kernels: 0 us -> 20.8 us
  other arithmetic: 7.93 us -> 25.2 us
  matrix products: 13.6 us -> 0 us
    all_gather x4 -> x2, waiting for transfers between devices: 425 us -> 9.54 us  [the longest x1 9.52 us: body(): heads_all = lax.all_gather(heads, 'x', axis=0)]
    reduce_scatter x1 -> x0, waiting for transfers between devices: 106 us -> none  [body(): lax.psum_scatter(term.astype(jnp.bfloat16), 'mp', scatter_dimension=0, ti...]
    psum x1 -> x0, blocking collectives: 97.4 us -> none  [body(): grad_gain = lax.psum(local_gain, ('dp', 'mp'))]
    ppermute x0 -> x17, starting transfers between devices: none -> 69.5 us  [the longest x3 19.3 us: ring(): behind = lax.ppermute(behind, AXES, FORTH)]
    ppermute x0 -> x17, waiting for transfers between devices: none -> 31.6 us  [the longest x3 20.5 us: ring(): behind = lax.ppermute(behind, AXES, FORTH)]
    all_to_all x0 -> x3, starting transfers between devices: none -> 23.6 us  [the longest x1 15.8 us: body(): lax.all_to_all(jnp.broadcast_to(gain_nat[None], (32, 28, 128)), AXES, 0,...]
    pallas_call x0 -> x2, Pallas kernels: none -> 20.8 us  [the longest x1 12 us: backward(): pl.pallas_call(backward_kernel, out_shape=(jax.ShapeDtypeStruct((2, 192,...]
    all_to_all x0 -> x3, waiting for transfers between devices: none -> 13.6 us  [the longest x1 11.1 us: body(): lax.all_to_all(jnp.broadcast_to(gain_nat[None], (32, 28, 128)), AXES, 0,...]
  transfers between devices with their start and end apart: 5 -> 22, of which waited for: 5 -> 9; matrix products, arithmetic and copies ran while one was open for 1% -> 17% of each run, Pallas kernels for 0% -> 0%
where the time goes in v1:
time: 243 us; the launch traced here: 239 us
  starting transfers between devices  93.1 us (38%)
  waiting for transfers between devices  54.8 us (23%)
  local copies, waits for them, and re-layouts  30.2 us (12%)
  other arithmetic  25.2 us (10%)
  Pallas kernels  20.8 us (9%)
  between operations  15.4 us (6%)
    ppermute x3, waiting for transfers between devices, ring(): behind = lax.ppermute(behind, AXES, FORTH)  20.5 us
    ppermute x3, starting transfers between devices, ring(): behind = lax.ppermute(behind, AXES, FORTH)  19.3 us
    all_to_all x1, starting transfers between devices, body(): lax.all_to_all(jnp.broadcast_to(gain_nat[None], (32, 28, 128)), AXES, 0,...  15.8 us
    pallas_call x1, Pallas kernels, backward(): pl.pallas_call(backward_kernel, out_shape=(jax.ShapeDtypeStruct((2, 192,...  12 us
    all_to_all x1, waiting for transfers between devices, body(): lax.all_to_all(jnp.broadcast_to(gain_nat[None], (32, 28, 128)), AXES, 0,...  11.1 us
    all_gather x1, waiting for transfers between devices, body(): heads_all = lax.all_gather(heads, 'x', axis=0)  9.52 us
    ppermute x3, starting transfers between devices, ring(): ahead = lax.ppermute(ahead, AXES, BACK)  8.86 us
    pallas_call x1, Pallas kernels, forward(): pl.pallas_call(forward_kernel, out_shape=jax.ShapeDtypeStruct((2, 192, 10...  8.83 us
  transfers between devices with their start and end apart: 22, of which 9 were waited for; matrix products, arithmetic and copies ran while one was open for 17% of the time, Pallas kernels for 0%

profile of v1, /device:TPU:1, one launch (start us, length us, event | category | flops | bytes accessed | tf_op | source)
XLA Modules:
  0.0 239.5 jit_solution(7414300354407091304)
XLA Ops:
  7.2 0.8 reshape.157
  8.8 2.4 %gather_fusion = bf16[48,3584]{1,0:T(8,128)(2,1)S(1)} fusion(bf16[128,3584]{1,0:T(8,128)(2,1)} %param.11, s32[1024]{0:T(1024)S(1)} %pad_clamp_fusion.2), kind=kCustom, calls=%fused_computation | custom fusion | bytes 688320 | tf_op jit(solution)/shard_map/gather | solution.py:189
  13.0 0.9 copy.21
  14.0 8.8 %collective-permute-start.2 = (bf16[64,512]{1,0:T(8,128)(2,1)S(1)}, bf16[64,512]{1,0:T(8,128)(2,1)S(1)}, u32[]{:S(2)}, u32[]{:S(2)}) collective-permute-start(bf16[64,512]{1,0:T(8,128)(2,1)S(1)} %broadcast_select_fusion.2), channel_id=1, source_target_pairs={{0,8},{8,0},{2,10},{10,2},{4,12},{12,4},{6,14},{14,6},{16,24},{24,... | collective-permute-start | bytes 196616 | tf_op jit(solution)/shard_map/ppermute | solution.py:177
  22.8 1.7 gather_fusion.4
  24.5 1.7 gather_fusion.3
  26.2 1.1 broadcast_in_dim.18
  27.3 3.6 %all-to-all-start = ((bf16[8,128,512]{2,1,0:T(8,128)(2,1)}), bf16[8,128,512]{2,1,0:T(8,128)(2,1)S(1)}, u32[]{:S(2)}, u32[]{:S(2)}) async-start(bf16[8,128,512]{2,1,0:T(8,128)(2,1)} %broadcast_in_dim.18), calls=%async_computation | async-start | bytes 2097152 | tf_op jit(solution)/shard_map/all_to_all | solution.py:203
  30.9 1.8 pad_maximum_fusion.2
  32.7 8.5 %collective-permute-start = (bf16[192,1024]{1,0:T(8,128)(2,1)}, bf16[192,1024]{1,0:T(8,128)(2,1)}, u32[]{:S(2)}, u32[]{:S(2)}) collective-permute-start(bf16[192,1024]{1,0:T(8,128)(2,1)} %pad_maximum_fusion.2), channel_id=1, source_target_pairs={{0,1},{1,0},{2,3},{3,2},{4,5},{5,4},{6,7},{7,6},{8,9},{9,8},{10,11... | collective-permute-start | bytes 1179656 | tf_op jit(solution)/shard_map/ppermute | solution.py:186
  41.3 1.7 gather_fusion.1
  42.9 1.7 gather_fusion.2
  44.6 0.9 constant_dynamic-update-slice_fusion.1
  45.6 1.0 constant_dynamic-update-slice_fusion
  46.5 8.7 %collective-permute-done = bf16[192,1024]{1,0:T(8,128)(2,1)} collective-permute-done((bf16[192,1024]{1,0:T(8,128)(2,1)}, bf16[192,1024]{1,0:T(8,128)(2,1)}, u32[]{:S(2)}, u32[]{:S(2)}) %collective-permute-start) | collective-permute-done | bytes 393248 | tf_op jit(solution)/shard_map/ppermute | solution.py:186
  55.2 1.1 broadcast_select_fusion.1
  56.3 0.7 fusion.21
  57.7 0.8 pad_maximum_fusion.3
  58.9 11.8 %collective-permute-start.6 = (bf16[1024,512]{1,0:T(8,128)(2,1)S(1)}, bf16[1024,512]{1,0:T(8,128)(2,1)}, u32[]{:S(2)}, u32[]{:S(2)}) collective-permute-start(bf16[1024,512]{1,0:T(8,128)(2,1)S(1)} %bitcast_select_fusion.refs_0_), channel_id=1, source_target_pairs={{0,64},{8,24},{2,66},{10,26},{4,68},{12,28},{6,70},{14,30},{16,80}... | collective-permute-start | bytes 3145736 | tf_op jit(solution)/shard_map/ppermute | solution.py:53
  70.8 1.9 collective-permute-start.3
  72.7 9.8 %collective-permute-done.6.refs_7_ = bf16[1024,512]{1,0:T(8,128)(2,1)} collective-permute-done((bf16[1024,512]{1,0:T(8,128)(2,1)S(1)}, bf16[1024,512]{1,0:T(8,128)(2,1)}, u32[]{:S(2)}, u32[]{:S(2)}) %collective-permute-start.6) | collective-permute-done | bytes 1048608 | tf_op jit(solution)/shard_map/ppermute | solution.py:53
  82.5 4.2 %collective-permute-start.7 = (bf16[1024,512]{1,0:T(8,128)(2,1)}, bf16[1024,512]{1,0:T(8,128)(2,1)}, u32[]{:S(2)}, u32[]{:S(2)}) collective-permute-start(bf16[1024,512]{1,0:T(8,128)(2,1)} %collective-permute-done.6.refs_7_), channel_id=1, source_target_pairs={{0,64},{8,24},{2,66},{10,26},{4,68},{12,28},{6,70},{14,30},{16,80}... | collective-permute-start | bytes 3145736 | tf_op jit(solution)/shard_map/ppermute | solution.py:53
  86.7 2.7 %collective-permute-start.4 = (bf16[1024,512]{1,0:T(8,128)(2,1)S(1)}, bf16[1024,512]{1,0:T(8,128)(2,1)}, u32[]{:S(2)}, u32[]{:S(2)}) collective-permute-start(bf16[1024,512]{1,0:T(8,128)(2,1)S(1)} %collective-permute-done.3.refs_1_), channel_id=1, source_target_pairs={{0,448},{8,57},{2,450},{10,59},{4,452},{12,61},{6,454},{14,63},{16... | collective-permute-start | bytes 3145736 | tf_op jit(solution)/shard_map/ppermute | solution.py:54
  89.5 9.5 %all-gather.6.cloned.1.call-done = bf16[768,1024]{1,0:T(8,128)(2,1)} async-done(((bf16[192,1024]{1,0:T(8,128)(2,1)}), bf16[768,1024]{1,0:T(8,128)(2,1)}) %all-gather.6.cloned.1.call-update) | async-done | bytes 1572880 | tf_op jit(solution)/shard_map/all_gather | solution.py:200
  99.0 3.8 %fusion.2 = (bf16[1,4,192,1024]{3,2,1,0:T(8,128)(2,1)}, bf16[4,192,1024]{2,1,0:T(8,128)(2,1)}) fusion(bf16[4,192,1024]{2,1,0:T(8,128)(2,1)} %bitcast.83, pred[]{:T(512)S(6)} %eq.18, bf16[24,4,8,1024]{3,2,1,0:T(8,128)(2,1)} %bitcast.82), kind=kLoop, calls=%fused_computation.10 | loop fusion | flops 1572864 | bytes 6291457 | tf_op jit(solution)/shard_map/stack | solution.py:213
  102.8 2.6 %collective-permute-start.1 = (bf16[4,192,1024]{2,1,0:T(8,128)(2,1)}, bf16[4,192,1024]{2,1,0:T(8,128)(2,1)}, u32[]{:S(2)}, u32[]{:S(2)}) collective-permute-start(bf16[4,192,1024]{2,1,0:T(8,128)(2,1)} %get-tuple-element.9), channel_id=1, source_target_pairs={{0,8},{8,0},{2,10},{10,2},{4,12},{12,4},{6,14},{14,6},{16,24},{24,... | collective-permute-start | bytes 4718600 | tf_op jit(solution)/shard_map/ppermute | solution.py:213
  105.3 3.3 %collective-permute-start.8 = (bf16[1024,512]{1,0:T(8,128)(2,1)}, bf16[1024,512]{1,0:T(8,128)(2,1)S(1)}, u32[]{:S(2)}, u32[]{:S(2)}) collective-permute-start(bf16[1024,512]{1,0:T(8,128)(2,1)} %collective-permute-done.7.refs_6_), channel_id=1, source_target_pairs={{0,64},{8,24},{2,66},{10,26},{4,68},{12,28},{6,70},{14,30},{16,80}... | collective-permute-start | bytes 3145736 | tf_op jit(solution)/shard_map/ppermute | solution.py:53
  108.6 4.2 %collective-permute-start.5 = (bf16[1024,512]{1,0:T(8,128)(2,1)}, bf16[1024,512]{1,0:T(8,128)(2,1)S(1)}, u32[]{:S(2)}, u32[]{:S(2)}) collective-permute-start(bf16[1024,512]{1,0:T(8,128)(2,1)} %collective-permute-done.4.refs_2_), channel_id=1, source_target_pairs={{0,448},{8,57},{2,450},{10,59},{4,452},{12,61},{6,454},{14,63},{16... | collective-permute-start | bytes 3145736 | tf_op jit(solution)/shard_map/ppermute | solution.py:54
  112.9 10.7 %collective-permute-done.8.refs_5_ = bf16[1024,512]{1,0:T(8,128)(2,1)S(1)} collective-permute-done((bf16[1024,512]{1,0:T(8,128)(2,1)}, bf16[1024,512]{1,0:T(8,128)(2,1)S(1)}, u32[]{:S(2)}, u32[]{:S(2)}) %collective-permute-start.8) | collective-permute-done | bytes 1048608 | tf_op jit(solution)/shard_map/ppermute | solution.py:53
  123.6 0.9 slice.54
  124.5 1.9 collective-permute-start.9
  126.5 0.9 slice.55
  127.3 4.6 %collective-permute-start.10 = (bf16[512,512]{1,0:T(8,128)(2,1)}, bf16[512,512]{1,0:T(8,128)(2,1)}, u32[]{:S(2)}, u32[]{:S(2)}) collective-permute-start(bf16[512,512]{1,0:T(8,128)(2,1)} %slice.55), channel_id=1, source_target_pairs={{0,448},{8,57},{2,450},{10,59},{4,452},{12,61},{6,454},{14,63},{16... | collective-permute-start | bytes 1572872 | tf_op jit(solution)/shard_map/ppermute | solution.py:58
  132.0 3.8 %pad_maximum_fusion.a_ref = bf16[2,4,192,1024]{3,2,1,0:T(8,128)(2,1)} fusion(bf16[1,4,192,1024]{3,2,1,0:T(8,128)(2,1)} %bitcast.10, bf16[1,4,192,1024]{3,2,1,0:T(8,128)(2,1)} %get-tuple-element.8), kind=kLoop, calls=%fused_computation.6 | loop fusion | flops 1572864 | bytes 6291456 | tf_op jit(solution)/shard_map/stack | solution.py:213
  136.2 1.1 constant_dynamic-update-slice_fusion.3
  137.3 1.0 collective-permute-done.10
  138.3 1.1 constant_dynamic-update-slice_fusion.2.refs_4_
  139.4 8.8 %forward.1.pred = f32[2,192,1024]{2,1,0:T(8,128)} custom-call(s32[2]{0:T(128)S(1)} %pad_add_fusion.meta, bf16[2,4,192,1024]{3,2,1,0:T(8,128)(2,1)} %pad_maximum_fusion.a_ref, bf16[1024,512]{1,0:T(8,128)(2,1)S(1)} %bitcast_select_fusion.refs_0_, bf16[1024,512]{1,0:T(8,128)(2,1)S(1)} %copy-done.4, bf16[1024,512]{1,0:T(8,128)(2,1)} %collective-permute-done.4.refs_2_, ...), custom_call_target="tpu_custom_call" | custom-call | flops 3221225472 | bytes 13631488 | tf_op jit(solution)/shard_map/forward/pallas_call | solution.py:133
  148.3 7.1 %collective-permute-start.11 = (f32[2,192,1024]{2,1,0:T(8,128)}, f32[2,192,1024]{2,1,0:T(8,128)}, u32[]{:S(2)}, u32[]{:S(2)}) collective-permute-start(f32[2,192,1024]{2,1,0:T(8,128)} %forward.1.pred), channel_id=1, source_target_pairs={{8,0},{10,2},{12,4},{14,6},{24,16},{26,18},{28,20},{30,22},{40,32}... | collective-permute-start | bytes 4718600 | tf_op jit(solution)/shard_map/ppermute | solution.py:217
  155.4 1.0 fusion.18
  156.4 2.0 collective-permute-start.12
  158.4 0.9 collective-permute-done.12
  159.4 1.2 pad_maximum_fusion.1.res
  160.6 1.2 copy-done.5
  161.8 12.0 %backward.1 = (bf16[2,192,3584]{2,1,0:T(8,128)(2,1)}, f32[8,512]{1,0:T(8,128)S(1)}) custom-call(bf16[2,4,192,1024]{3,2,1,0:T(8,128)(2,1)} %pad_maximum_fusion.a_ref, f32[2,192,1024]{2,1,0:T(8,128)} %forward.1.pred, f32[2,192,1024]{2,1,0:T(8,128)} %collective-permute-done.11.att, bf16[2,192,1024]{2,1,0:T(8,128)(2,1)S(1)} %pad_maximum_fusion.1.res, ...), custom_call_target="tpu_custom_call" | custom-call | flops 3221225472 | bytes 16777216 | tf_op jit(solution)/shard_map/backward/pallas_call | solution.py:146
  173.8 2.5 %dynamic-slice_bitcast_fusion.2 = (bf16[2,48,3584]{2,1,0:T(8,128)(2,1)S(1)}, bf16[2,48,3584]{2,1,0:T(8,128)(2,1)}, bf16[2,48,3584]{2,1,0:T(8,128)(2,1)S(1)}) fusion(bf16[2,4,48,3584]{3,2,1,0:T(8,128)(2,1)} %bitcast.78, s32[]{:T(128)S(6)} %select_n.196, s32[]{:T(128)S(6)} %select_n.200, s32[]{:T(128)S(6)} %select_n.198), kind=kLoop, calls=%fused_computation.27 | loop fusion | bytes 4128780 | tf_op jit(solution)/shard_map/jit(dynamic_index_in_dim)/squeeze | solution.py:223
  176.3 1.5 collective-permute-start.15
  177.8 1.5 collective-permute-start.14
  179.4 1.5 collective-permute-start.13
  181.0 0.9 broadcast_in_dim.21
  181.9 15.8 %all-to-all-start.1 = ((f32[32,28,128]{2,1,0:T(8,128)}), f32[32,28,128]{2,1,0:T(8,128)S(1)}, u32[]{:S(2)}, u32[]{:S(2)}) async-start(f32[32,28,128]{2,1,0:T(8,128)} %broadcast_in_dim.21), calls=%async_computation.1 | async-start | bytes 1048576 | tf_op jit(solution)/shard_map/all_to_all | solution.py:234
  197.7 2.0 convert_add_fusion
  199.8 0.8 fusion.8
  200.5 1.3 collective-permute-start.16
  201.8 11.1 %all-to-all-done.1 = f32[32,28,128]{2,1,0:T(8,128)S(1)} async-done(((f32[32,28,128]{2,1,0:T(8,128)}), f32[32,28,128]{2,1,0:T(8,128)S(1)}, u32[]{:S(2)}, u32[]{:S(2)}) %all-to-all-start.1) | async-done | bytes 458784 | tf_op jit(solution)/shard_map/all_to_all | solution.py:234
  213.0 0.7 broadcast_in_dim.22
  213.7 4.2 %all-to-all-start.2 = ((f32[16,28,128]{2,1,0:T(8,128)}), f32[16,28,128]{2,1,0:T(8,128)}, u32[]{:S(2)}, u32[]{:S(2)}) async-start(f32[16,28,128]{2,1,0:T(8,128)} %broadcast_in_dim.22), calls=%async_computation.2 | async-start | bytes 524288 | tf_op jit(solution)/shard_map/all_to_all | solution.py:238
  217.9 2.0 fusion.4
  219.9 1.5 reshape.166
  221.4 2.0 multiply_reduce_fusion
  223.4 1.4 reshape.167
  224.9 2.4 %scatter_custom_fusion = bf16[128,3584]{1,0:T(8,128)(2,1)} fusion(s32[48]{0:T(128)} %copy-done.19, bf16[]{:T(256)} %constant.124.clone.1, f32[48,3584]{1,0:T(8,128)S(1)} %reshape.167, f32[]{:T(128)} %constant.135.clone.1, f32[48]{0:T(128)S(1)} %get-tuple-element.6, f32[3584]{0:T(1024)S(1)} %copy-done.16, f32[48]{0:T(128)S(1)} %copy-done.18, ...), kind=kCustom, calls=%fused_computation.29 | custom fusion | flops 1720320 | bytes 1965440 | tf_op jit(solution)/shard_map/scatter | solution.py:247
  227.3 2.5 %all-to-all-done.2 = f32[16,28,128]{2,1,0:T(8,128)} async-done(((f32[16,28,128]{2,1,0:T(8,128)}), f32[16,28,128]{2,1,0:T(8,128)}, u32[]{:S(2)}, u32[]{:S(2)}) %all-to-all-start.2) | async-done | bytes 229408 | tf_op jit(solution)/shard_map/all_to_all | solution.py:238
  229.8 1.0 reduce_sum.48
  (84 shorter events, 5.8 us)
Async XLA Ops:
  7.2 17.3 %copy-start = (bf16[1024,512]{1,0:T(8,128)(2,1)S(1)}, bf16[1024,512]{1,0:T(8,128)(2,1)}, u32[]{:S(2)}) copy-start(bf16[1024,512]{1,0:T(8,128)(2,1)} %param.7) | copy-start | bytes 3145732
  7.2 82.3 %all-gather.4.cloned.1.call-start = ((), (), s32[]{:S(2)}) async-start(), calls=%async_computation.3 | async-start | bytes 1966080 | tf_op jit(solution)/shard_map/all_gather | solution.py:193
  8.3 0.5 copy-start.19
  8.8 3.0 %copy-start.15 = (f32[3584]{0:T(1024)S(1)}, f32[3584]{0:T(1024)}, u32[]{:S(2)}) copy-start(f32[3584]{0:T(1024)} %param.12) | copy-start | bytes 43012
  11.6 0.9 copy-start.7
  11.9 0.6 copy-start.14
  11.9 0.6 copy-start.17
  12.7 1.3 copy-start.12
  12.7 1.3 copy-start.13
  12.7 10.1 %copy-start.6 = (bf16[1024,512]{1,0:T(8,128)(2,1)S(1)}, bf16[1024,512]{1,0:T(8,128)(2,1)}, u32[]{:S(2)}) copy-start(bf16[1024,512]{1,0:T(8,128)(2,1)} %param.9) | copy-start | bytes 3145732
  14.0 12.2 %collective-permute-start.2 = (bf16[64,512]{1,0:T(8,128)(2,1)S(1)}, bf16[64,512]{1,0:T(8,128)(2,1)S(1)}, u32[]{:S(2)}, u32[]{:S(2)}) collective-permute-start(bf16[64,512]{1,0:T(8,128)(2,1)S(1)} %broadcast_select_fusion.2), channel_id=1, source_target_pairs={{0,8},{8,0},{2,10},{10,2},{4,12},{12,4},{6,14},{14,6},{16,24},{24,... | collective-permute-start | bytes 196616 | tf_op jit(solution)/shard_map/ppermute | solution.py:177
  27.3 31.2 %all-to-all-start = ((bf16[8,128,512]{2,1,0:T(8,128)(2,1)}), bf16[8,128,512]{2,1,0:T(8,128)(2,1)S(1)}, u32[]{:S(2)}, u32[]{:S(2)}) async-start(bf16[8,128,512]{2,1,0:T(8,128)(2,1)} %broadcast_in_dim.18), calls=%async_computation | async-start | bytes 2097152 | tf_op jit(solution)/shard_map/all_to_all | solution.py:203
  30.9 68.1 %all-gather.6.cloned.1.call-start = ((), (), s32[]{:S(2)}) async-start(), calls=%async_computation.4 | async-start | bytes 1966080 | tf_op jit(solution)/shard_map/all_gather | solution.py:200
  32.7 22.5 %collective-permute-start = (bf16[192,1024]{1,0:T(8,128)(2,1)}, bf16[192,1024]{1,0:T(8,128)(2,1)}, u32[]{:S(2)}, u32[]{:S(2)}) collective-permute-start(bf16[192,1024]{1,0:T(8,128)(2,1)} %pad_maximum_fusion.2), channel_id=1, source_target_pairs={{0,1},{1,0},{2,3},{3,2},{4,5},{5,4},{6,7},{7,6},{8,9},{9,8},{10,11... | collective-permute-start | bytes 1179656 | tf_op jit(solution)/shard_map/ppermute | solution.py:186
  58.9 23.6 %collective-permute-start.6 = (bf16[1024,512]{1,0:T(8,128)(2,1)S(1)}, bf16[1024,512]{1,0:T(8,128)(2,1)}, u32[]{:S(2)}, u32[]{:S(2)}) collective-permute-start(bf16[1024,512]{1,0:T(8,128)(2,1)S(1)} %bitcast_select_fusion.refs_0_), channel_id=1, source_target_pairs={{0,64},{8,24},{2,66},{10,26},{4,68},{12,28},{6,70},{14,30},{16,80}... | collective-permute-start | bytes 3145736 | tf_op jit(solution)/shard_map/ppermute | solution.py:53
  70.8 15.9 %collective-permute-start.3 = (bf16[1024,512]{1,0:T(8,128)(2,1)S(1)}, bf16[1024,512]{1,0:T(8,128)(2,1)S(1)}, u32[]{:S(2)}, u32[]{:S(2)}) collective-permute-start(bf16[1024,512]{1,0:T(8,128)(2,1)S(1)} %bitcast_select_fusion.refs_0_), channel_id=1, source_target_pairs={{0,448},{8,57},{2,450},{10,59},{4,452},{12,61},{6,454},{14,63},{16... | collective-permute-start | bytes 3145736 | tf_op jit(solution)/shard_map/ppermute | solution.py:54
  82.5 22.8 %collective-permute-start.7 = (bf16[1024,512]{1,0:T(8,128)(2,1)}, bf16[1024,512]{1,0:T(8,128)(2,1)}, u32[]{:S(2)}, u32[]{:S(2)}) collective-permute-start(bf16[1024,512]{1,0:T(8,128)(2,1)} %collective-permute-done.6.refs_7_), channel_id=1, source_target_pairs={{0,64},{8,24},{2,66},{10,26},{4,68},{12,28},{6,70},{14,30},{16,80}... | collective-permute-start | bytes 3145736 | tf_op jit(solution)/shard_map/ppermute | solution.py:53
  86.7 16.0 %copy-start.3 = (bf16[1024,512]{1,0:T(8,128)(2,1)}, bf16[1024,512]{1,0:T(8,128)(2,1)S(1)}, u32[]{:S(2)}) copy-start(bf16[1024,512]{1,0:T(8,128)(2,1)S(1)} %collective-permute-done.3.refs_1_) | copy-start | bytes 3145732
  86.7 21.9 %collective-permute-start.4 = (bf16[1024,512]{1,0:T(8,128)(2,1)S(1)}, bf16[1024,512]{1,0:T(8,128)(2,1)}, u32[]{:S(2)}, u32[]{:S(2)}) collective-permute-start(bf16[1024,512]{1,0:T(8,128)(2,1)S(1)} %collective-permute-done.3.refs_1_), channel_id=1, source_target_pairs={{0,448},{8,57},{2,450},{10,59},{4,452},{12,61},{6,454},{14,63},{16... | collective-permute-start | bytes 3145736 | tf_op jit(solution)/shard_map/ppermute | solution.py:54
  102.8 29.2 %collective-permute-start.1 = (bf16[4,192,1024]{2,1,0:T(8,128)(2,1)}, bf16[4,192,1024]{2,1,0:T(8,128)(2,1)}, u32[]{:S(2)}, u32[]{:S(2)}) collective-permute-start(bf16[4,192,1024]{2,1,0:T(8,128)(2,1)} %get-tuple-element.9), channel_id=1, source_target_pairs={{0,8},{8,0},{2,10},{10,2},{4,12},{12,4},{6,14},{14,6},{16,24},{24,... | collective-permute-start | bytes 4718600 | tf_op jit(solution)/shard_map/ppermute | solution.py:213
  105.3 18.3 %collective-permute-start.8 = (bf16[1024,512]{1,0:T(8,128)(2,1)}, bf16[1024,512]{1,0:T(8,128)(2,1)S(1)}, u32[]{:S(2)}, u32[]{:S(2)}) collective-permute-start(bf16[1024,512]{1,0:T(8,128)(2,1)} %collective-permute-done.7.refs_6_), channel_id=1, source_target_pairs={{0,64},{8,24},{2,66},{10,26},{4,68},{12,28},{6,70},{14,30},{16,80}... | collective-permute-start | bytes 3145736 | tf_op jit(solution)/shard_map/ppermute | solution.py:53
  108.6 17.8 %collective-permute-start.5 = (bf16[1024,512]{1,0:T(8,128)(2,1)}, bf16[1024,512]{1,0:T(8,128)(2,1)S(1)}, u32[]{:S(2)}, u32[]{:S(2)}) collective-permute-start(bf16[1024,512]{1,0:T(8,128)(2,1)} %collective-permute-done.4.refs_2_), channel_id=1, source_target_pairs={{0,448},{8,57},{2,450},{10,59},{4,452},{12,61},{6,454},{14,63},{16... | collective-permute-start | bytes 3145736 | tf_op jit(solution)/shard_map/ppermute | solution.py:54
  123.6 2.8 %copy-start.9 = (bf16[1024,512]{1,0:T(8,128)(2,1)}, bf16[1024,512]{1,0:T(8,128)(2,1)S(1)}, u32[]{:S(2)}) copy-start(bf16[1024,512]{1,0:T(8,128)(2,1)S(1)} %collective-permute-done.8.refs_5_) | copy-start | bytes 3145732
  124.5 11.7 %collective-permute-start.9 = (bf16[512,512]{1,0:T(8,128)(2,1)}, bf16[512,512]{1,0:T(8,128)(2,1)}, u32[]{:S(2)}, u32[]{:S(2)}) collective-permute-start(bf16[512,512]{1,0:T(8,128)(2,1)} %slice.54), channel_id=1, source_target_pairs={{0,64},{8,24},{2,66},{10,26},{4,68},{12,28},{6,70},{14,30},{16,80}... | collective-permute-start | bytes 1572872 | tf_op jit(solution)/shard_map/ppermute | solution.py:57
  127.3 11.0 %collective-permute-start.10 = (bf16[512,512]{1,0:T(8,128)(2,1)}, bf16[512,512]{1,0:T(8,128)(2,1)}, u32[]{:S(2)}, u32[]{:S(2)}) collective-permute-start(bf16[512,512]{1,0:T(8,128)(2,1)} %slice.55), channel_id=1, source_target_pairs={{0,448},{8,57},{2,450},{10,59},{4,452},{12,61},{6,454},{14,63},{16... | collective-permute-start | bytes 1572872 | tf_op jit(solution)/shard_map/ppermute | solution.py:58
  135.8 3.6 %copy-start.4 = (bf16[1024,512]{1,0:T(8,128)(2,1)S(1)}, bf16[1024,512]{1,0:T(8,128)(2,1)}, u32[]{:S(2)}) copy-start(bf16[1024,512]{1,0:T(8,128)(2,1)} %copy-done.3) | copy-start | bytes 3145732
  139.4 8.9 %copy-start.1 = (bf16[1024,512]{1,0:T(8,128)(2,1)}, bf16[1024,512]{1,0:T(8,128)(2,1)S(1)}, u32[]{:S(2)}) copy-start(bf16[1024,512]{1,0:T(8,128)(2,1)S(1)} %constant_dynamic-update-slice_fusion.2.refs_4_) | copy-start | bytes 3145732
  139.4 15.9 %copy-start.10 = (bf16[192,512]{1,0:T(8,128)(2,1)S(1)}, bf16[192,512]{1,0:T(8,128)(2,1)}, u32[]{:S(2)}) copy-start(bf16[192,512]{1,0:T(8,128)(2,1)} %get-tuple-element.19) | copy-start | bytes 589828
  139.4 15.9 %copy-start.11 = (bf16[192,512]{1,0:T(8,128)(2,1)S(1)}, bf16[192,512]{1,0:T(8,128)(2,1)}, u32[]{:S(2)}) copy-start(bf16[192,512]{1,0:T(8,128)(2,1)} %get-tuple-element.17) | copy-start | bytes 589828
  148.3 12.3 %collective-permute-start.11 = (f32[2,192,1024]{2,1,0:T(8,128)}, f32[2,192,1024]{2,1,0:T(8,128)}, u32[]{:S(2)}, u32[]{:S(2)}) collective-permute-start(f32[2,192,1024]{2,1,0:T(8,128)} %forward.1.pred), channel_id=1, source_target_pairs={{8,0},{10,2},{12,4},{14,6},{24,16},{26,18},{28,20},{30,22},{40,32}... | collective-permute-start | bytes 4718600 | tf_op jit(solution)/shard_map/ppermute | solution.py:217
  156.4 3.0 %collective-permute-start.12 = (bf16[192,1024]{1,0:T(8,128)(2,1)}, bf16[192,1024]{1,0:T(8,128)(2,1)}, u32[]{:S(2)}, u32[]{:S(2)}) collective-permute-start(bf16[192,1024]{1,0:T(8,128)(2,1)} %get-tuple-element.16), channel_id=1, source_target_pairs={{8,0},{10,2},{12,4},{14,6},{24,16},{26,18},{28,20},{30,22},{40,32}... | collective-permute-start | bytes 1179656 | tf_op jit(solution)/shard_map/ppermute | solution.py:201
  158.4 2.1 copy-start.2
  160.6 1.2 copy-start.5
  176.3 21.4 %collective-permute-start.15 = (bf16[2,48,3584]{2,1,0:T(8,128)(2,1)}, bf16[2,48,3584]{2,1,0:T(8,128)(2,1)}, u32[]{:S(2)}, u32[]{:S(2)}) collective-permute-start(bf16[2,48,3584]{2,1,0:T(8,128)(2,1)} %get-tuple-element.11), channel_id=1, source_target_pairs={{0,6},{2,0},{4,2},{6,4},{16,22},{18,16},{20,18},{22,20},{32,38},{3... | collective-permute-start | bytes 2064392 | tf_op jit(solution)/shard_map/ppermute | solution.py:225
  177.8 19.9 %collective-permute-start.14 = (bf16[2,48,3584]{2,1,0:T(8,128)(2,1)S(1)}, bf16[2,48,3584]{2,1,0:T(8,128)(2,1)}, u32[]{:S(2)}, u32[]{:S(2)}) collective-permute-start(bf16[2,48,3584]{2,1,0:T(8,128)(2,1)S(1)} %get-tuple-element.12), channel_id=1, source_target_pairs={{0,4},{2,6},{4,0},{6,2},{16,20},{18,22},{20,16},{22,18},{32,36},{3... | collective-permute-start | bytes 2064392 | tf_op jit(solution)/shard_map/ppermute | solution.py:225
  179.4 18.3 %collective-permute-start.13 = (bf16[2,48,3584]{2,1,0:T(8,128)(2,1)S(1)}, bf16[2,48,3584]{2,1,0:T(8,128)(2,1)}, u32[]{:S(2)}, u32[]{:S(2)}) collective-permute-start(bf16[2,48,3584]{2,1,0:T(8,128)(2,1)S(1)} %get-tuple-element.10), channel_id=1, source_target_pairs={{0,2},{2,4},{4,6},{6,0},{16,18},{18,20},{20,22},{22,16},{32,34},{3... | collective-permute-start | bytes 2064392 | tf_op jit(solution)/shard_map/ppermute | solution.py:225
  181.9 31.1 %all-to-all-start.1 = ((f32[32,28,128]{2,1,0:T(8,128)}), f32[32,28,128]{2,1,0:T(8,128)S(1)}, u32[]{:S(2)}, u32[]{:S(2)}) async-start(f32[32,28,128]{2,1,0:T(8,128)} %broadcast_in_dim.21), calls=%async_computation.1 | async-start | bytes 1048576 | tf_op jit(solution)/shard_map/all_to_all | solution.py:234
  200.5 17.4 %collective-permute-start.16 = (bf16[48,3584]{1,0:T(8,128)(2,1)}, bf16[48,3584]{1,0:T(8,128)(2,1)}, u32[]{:S(2)}, u32[]{:S(2)}) collective-permute-start(bf16[48,3584]{1,0:T(8,128)(2,1)} %fusion.8), channel_id=1, source_target_pairs={{0,8},{2,10},{4,12},{6,14},{16,24},{18,26},{20,28},{22,30},{32,40}... | collective-permute-start | bytes 1032200 | tf_op jit(solution)/shard_map/ppermute | solution.py:228
  213.7 16.1 %all-to-all-start.2 = ((f32[16,28,128]{2,1,0:T(8,128)}), f32[16,28,128]{2,1,0:T(8,128)}, u32[]{:S(2)}, u32[]{:S(2)}) async-start(f32[16,28,128]{2,1,0:T(8,128)} %broadcast_in_dim.22), calls=%async_computation.2 | async-start | bytes 524288 | tf_op jit(solution)/shard_map/all_to_all | solution.py:238
  217.9 3.5 %copy-start.8 = (f32[48,8,448]{2,1,0:T(8,128)S(1)}, f32[48,8,448]{2,1,0:T(8,128)}, u32[]{:S(2)}) copy-start(f32[48,8,448]{2,1,0:T(8,128)} %copy-done.7) | copy-start | bytes 2064388
  221.4 3.5 %copy-start.16 = (f32[3584]{0:T(1024)S(1)}, f32[3584]{0:T(1024)}, u32[]{:S(2)}) copy-start(f32[3584]{0:T(1024)} %param.12) | copy-start | bytes 43012
  221.4 3.5 %copy-start.18 = (f32[48]{0:T(128)S(1)}, f32[48]{0:T(128)}, u32[]{:S(2)}) copy-start(f32[48]{0:T(128)} %copy-done.17) | copy-start | bytes 580
Sparse Core Ops, SparseCore 0:
  14.1 37.3 all-gather.3
  58.6 40.3 all-gather.5

commit v2 on v0

v2 whole, which is shorter than its diff:
```python
import jax
import jax.numpy as jnp
from jax import lax
from jax.experimental import pallas as pl
from jax.experimental.pallas import tpu as pltpu
from jax.sharding import Mesh
from jax.sharding import PartitionSpec as P

EPS = 1e-06
NY, NZL, NC, NX, NZH = 8, 4, 2, 4, 2
NZ = NZL * NZH
AXES = ("y", "zl", "c", "x", "zh")
F32 = jnp.float32
BF16 = jnp.bfloat16
NT = (((1,), (1,)), ((), ()))


def dev(y, z, c, x):
    return (((y * NZL + z % NZL) * NC + c) * NX + x) * NZH + z // NZL


CHIPS = [(y, z, x) for y in range(NY) for z in range(NZ) for x in range(NX)]
Z_ON_0 = [[dev(y, z, 0, x) for z in range(NZ)] for y in range(NY) for x in range(NX)] + [
    [dev(y, z, 1, x) for y in range(NY)] for z in range(NZ) for x in range(NX)
]
Y_ON_0 = [[dev(y, z, 0, x) for y in range(NY)] for z in range(NZ) for x in range(NX)] + [
    [dev(y, z, 1, x) for z in range(NZ)] for y in range(NY) for x in range(NX)
]
FIRST = [
    [dev(h * 4 + y, z, c, x) for x in range(NX) for y in range(4)]
    for h in range(2)
    for z in range(NZ)
    for c in range(NC)
]
SECOND = [
    [dev(h * 4 + y, z, c, x) for h in range(2) for z in range(NZ)]
    for c in range(NC)
    for x in range(NX)
    for y in range(4)
]
SWAP = [(0, 1), (1, 0)]

VMEM = pl.BlockSpec(memory_space=pltpu.VMEM)
SMEM = pl.BlockSpec(memory_space=pltpu.SMEM)
ANY = pl.BlockSpec(memory_space=pl.ANY)
PARAMS = pltpu.CompilerParams(vmem_limit_bytes=48 * 1024 * 1024)


def call(kernel, outs, ins, scratch, flops, nbytes, name):
    return pl.pallas_call(
        kernel,
        out_shape=[jax.ShapeDtypeStruct(shape, kind) for shape, kind in outs],
        in_specs=ins,
        out_specs=[VMEM] * len(outs),
        scratch_shapes=scratch,
        compiler_params=PARAMS,
        cost_estimate=pl.CostEstimate(flops=flops, bytes_accessed=nbytes, transcendentals=0),
        name=name,
    )


def hot_rows(idx, b):
    return (lax.broadcasted_iota(jnp.int32, (48, 128), 1) + b * 128 == idx[b]).astype(BF16)


def pick_rows(meta, idx, context, residual, mine, theirs):
    for b in range(8):
        x, zh = b // NZH, b % NZH
        hot = hot_rows(idx, b)
        for part, ref in enumerate((context, residual)):
            rows = jnp.dot(hot, ref[b * 128 : b * 128 + 128, :], preferred_element_type=F32).astype(BF16)
            at = (slice(x * 48, x * 48 + 48), slice(part * 512, part * 512 + 512))

            @pl.when(meta[1] == zh)
            def _():
                mine[at] = rows

            @pl.when(meta[1] != zh)
            def _():
                theirs[at] = rows


def norm_rows(meta, idx, hidden, gain, hid_out, normed_out):
    hid = jnp.dot(hot_rows(idx, meta[2]), hidden[...], preferred_element_type=F32)
    hid_out[...] = hid.astype(BF16)
    stat = lax.rsqrt(jnp.mean(hid * hid, axis=1, keepdims=True) + EPS)
    normed_out[...] = (hid * stat * gain[...]).astype(BF16)


def pair_rows(meta, got, proj, outp, out):
    @pl.when(meta[3] == 0)
    def _():
        for i in range(8):
            out[i, 0, :56, :] = proj[...]
            out[i, 0, 56:, :] = jnp.zeros((8, 512), BF16)
            out[i, 1] = got[...]

    @pl.when(meta[3] != 0)
    def _():
        for i in range(8):
            out[i, 0] = got[...]
            out[i, 1] = outp[...]


def tighten(meta, lines, out):
    @pl.when(meta[3] == 0)
    def _():
        for h in range(NZH):
            for i in range(8):
                row = h * 512 + i * 56
                out[row : row + 56, :] = lines[h * 4 + i // 2, i % 2, :56, :]
            out[h * 512 + 448 : h * 512 + 512, :] = jnp.zeros((64, 512), BF16)

    @pl.when(meta[3] != 0)
    def _():
        for i in range(16):
            out[i * 64 : i * 64 + 64, :] = lines[i // 2, i % 2]


def join(meta, here, other, heads, res):
    def put(zh, low, high):
        @pl.when(meta[1] == zh)
        def _():
            heads[:, :512], heads[:, 512:] = low[:, :512], high[:, :512]
            res[:, :512], res[:, 512:] = low[:, 512:], high[:, 512:]

    put(0, here, other)
    put(1, other, here)


def choose(meta, *refs):
    normed, heads, (keep, give) = refs[0], refs[1 : 1 + NX], refs[1 + NX :]

    def put(core, to_normed, to_heads):
        @pl.when(meta[3] == core)
        def _():
            for y in range(NY):
                to_normed[:, y * 512 : y * 512 + 448] = normed[:, y * 448 : y * 448 + 448]
                to_normed[:, y * 512 + 448 : y * 512 + 512] = jnp.zeros((192, 64), BF16)
            for d in range(NX):
                x = (meta[4] + d) % NX
                to_heads[:, pl.ds(pl.multiple_of(x * 1024, 1024), 1024)] = heads[d][...]

    put(0, keep, give)
    put(1, give, keep)


def load(w, buf, sems):
    copies = [pltpu.make_async_copy(w.at[k], buf.at[k], sems.at[k]) for k in range(8)]
    for copy in copies:
        copy.start()
    return copies


def forward(meta, own, oth, w, out, teach, buf, sems):
    copies = load(w, buf, sems)
    out[...] = jnp.zeros_like(out)

    def part(lanes):
        pieces = [jnp.concatenate([ref[:, lane] for lane in lanes], axis=1) for ref in (own, oth)]
        return jnp.concatenate(pieces, axis=0)

    for k in range(8):
        copies[k].wait()

        @pl.when(meta[3] == 0)
        def _():
            a = part([slice(k * 512, k * 512 + 512)])
            for h in range(NZH):
                cols = slice(h * 512, h * 512 + 512)
                out[:, cols] += jnp.dot(a, buf[k, cols, :], preferred_element_type=F32)

        @pl.when(meta[3] != 0)
        def _():
            a = part([slice(y * 512 + k % NZL * 128, y * 512 + k % NZL * 128 + 128) for y in range(NY)])
            cols = slice(k // NZL * 512, k // NZL * 512 + 512)
            out[:, cols] += jnp.dot(a, buf[k], preferred_element_type=F32)

    teach[:192] = out[192:].astype(BF16)
    teach[192:] = out[:192].astype(BF16)


def backward(meta, pred, teach, res_own, res_oth, own, oth, gain, w, term_own, term_oth, gain_out, g_buf, buf, sems):
    copies = load(w, buf, sems)
    g_buf[:192] = (pred[:192] - (res_own[...].astype(F32) + teach[:192].astype(F32))).astype(BF16)
    g_buf[192:] = (pred[192:] - (res_oth[...].astype(F32) + teach[192:].astype(F32))).astype(BF16)
    for y in range(NY):
        copies[y].wait()
        cols = slice(y * 448, y * 448 + 448)
        lanes = slice(y * 512, y * 512 + 448)
        term = lax.dot_general(g_buf[:, :512], buf[y, :448, :], NT, preferred_element_type=F32)
        term = term + lax.dot_general(g_buf[:, 512:], buf[y, 512:960, :], NT, preferred_element_type=F32)
        a = jnp.concatenate([own[:, lanes], oth[:, lanes]], axis=0).astype(F32)
        total = jnp.sum(term * a, axis=0, keepdims=True) / gain[:, cols]
        gain_out[:, cols] = jnp.where(meta[3] == 0, total, 0.0)
        term = term.astype(BF16)
        term_own[:, cols] = term[:192]
        term_oth[:, cols] = term[192:]


def finish(meta, idx, part0, part1, part2, part3, hid_ref, gain_ref, out):
    gain = gain_ref[...]
    hid = hid_ref[...].astype(F32)
    scaled = (part0[...].astype(F32) + part1[...].astype(F32)) + (part2[...].astype(F32) + part3[...].astype(F32))
    scaled = scaled * gain
    width = hid.shape[1]
    stat = lax.rsqrt(jnp.mean(hid * hid, axis=1, keepdims=True) + EPS)
    inner = jnp.sum(hid * scaled, axis=1, keepdims=True)
    rows = (stat * scaled - hid * (stat * stat * stat * inner / width)).astype(BF16)
    m = meta[2]
    own = idx[:, :48]
    for b in range(1, 8):
        own = jnp.where(m == b, idx[:, b * 48 : b * 48 + 48] - b * 128, own)
    hot = (lax.broadcasted_iota(jnp.int32, (128, 48), 0) == own).astype(BF16)
    out[...] = jnp.dot(hot, rows, preferred_element_type=F32).astype(BF16)


def spread(block, axis, size, groups=None):
    return lax.all_to_all(
        jnp.broadcast_to(block[None], (size,) + block.shape), axis, 0, 0, axis_index_groups=groups
    )


def body(context, w_out, residual, w_proj, hidden, gain, matched):
    width = hidden.shape[1]
    own_rows = hidden.shape[0]
    c, x, zh = (lax.axis_index(name) for name in ("c", "x", "zh"))
    z = zh * NZL + lax.axis_index("zl")
    m = x * NZH + zh
    meta = jnp.stack([z, zh, m, c, x]).astype(jnp.int32)
    idx, idx_row = matched.reshape(8, 48, 1), matched.reshape(1, matched.shape[0])
    gain_row = gain.reshape(1, width)
    first = c == 0

    hid, normed = call(
        norm_rows,
        [((48, width), BF16), ((48, width), BF16)],
        [SMEM] + [VMEM] * 3,
        [],
        2 * 48 * 128 * width,
        2 << 20,
        "norm",
    )(meta, idx, hidden, gain_row)
    normed = lax.all_gather(normed, "x", axis=0, tiled=True)

    got = lax.ppermute(jnp.where(first, w_out, jnp.pad(w_proj, ((0, 8), (0, 0)))), "c", SWAP)
    (pair,) = call(
        pair_rows, [((8, 2, 64, 512), BF16)], [SMEM] + [VMEM] * 3, [], 0, 2 << 20, "pair"
    )(meta, got, w_proj, w_out)
    lines = lax.all_to_all(pair, AXES, 0, 0, axis_index_groups=Z_ON_0)
    (line,) = call(tighten, [((1024, 512), BF16)], [SMEM, VMEM], [], 0, 2 << 20, "tighten")(meta, lines)

    here, away = call(
        pick_rows, [((192, 1024), BF16)] * 2, [SMEM] + [VMEM] * 3, [], 2 * 384 * 128 * 1024, 3 << 20, "pick"
    )(meta, idx, context, residual)
    line, away, normed = lax.optimization_barrier((line, away, normed))
    w = lax.all_gather(line, AXES, axis=0, tiled=True, axis_index_groups=Y_ON_0).reshape(8, 1024, 512)

    heads, res_own = call(
        join, [((192, 1024), BF16)] * 2, [SMEM, VMEM, VMEM], [], 0, 3 << 20, "join"
    )(meta, here, lax.ppermute(away, "zh", SWAP))
    res_oth = lax.ppermute(res_own, AXES, [(dev(y, z, 1, x), dev(y, z, 0, x)) for y, z, x in CHIPS])

    heads = [heads] + [lax.ppermute(heads, "x", [(i, (i - d) % NX) for i in range(NX)]) for d in range(1, NX)]
    keep, give = call(
        choose, [((192, 4096), BF16)] * 2, [SMEM] + [VMEM] * 5, [], 0, 6 << 20, "choose"
    )(meta, normed, *heads)
    give, res_oth = lax.optimization_barrier((give, res_oth))
    taken = lax.ppermute(give, "c", SWAP)

    wbuf = [pltpu.VMEM((8, 1024, 512), BF16), pltpu.SemaphoreType.DMA((8,))]
    pred, teach = call(
        forward,
        [((384, 1024), F32), ((384, 1024), BF16)],
        [SMEM] + [VMEM] * 2 + [ANY],
        wbuf,
        2 * 384 * 4096 * 1024,
        13 << 20,
        "forward",
    )(meta, keep, taken, w)
    teach = lax.ppermute(teach, AXES, [(dev(y, z, 1, x), dev(y, z, 0, x)) for y, z, x in CHIPS])
    term_own, term_oth, gain_part = call(
        backward,
        [((192, width), BF16), ((192, width), BF16), ((1, width), F32)],
        [SMEM] + [VMEM] * 7 + [ANY],
        [pltpu.VMEM((384, 1024), BF16)] + wbuf,
        2 * 384 * width * 1024,
        16 << 20,
        "backward",
    )(meta, pred, teach, res_own, res_oth, keep, taken, gain_row, w)

    gain_wide = jnp.broadcast_to(gain_part.reshape(1, 28, 128), (16, 28, 128))
    gain_wide, term_oth = lax.optimization_barrier((gain_wide, term_oth))
    gain_part = jnp.sum(lax.all_to_all(gain_wide, AXES, 0, 0, axis_index_groups=FIRST), axis=0)

    handed = lax.ppermute(term_oth, AXES, [(dev(y, z, 0, x), dev(y, z, 1, x)) for y, z, x in CHIPS])
    summed = jnp.where(first, term_own, handed).reshape(NX, 48, width)
    parts = [lax.dynamic_index_in_dim(summed, (x + d) % NX, 0, keepdims=False) for d in range(NX)]
    gain_part, parts[0] = lax.optimization_barrier((gain_part, parts[0]))
    for d in range(1, NX):
        parts[d] = lax.ppermute(parts[d], "x", [(i, (i + d) % NX) for i in range(NX)])
    (grad_hidden,) = call(
        finish, [((own_rows, width), BF16)], [SMEM] + [VMEM] * 7, [], 1 << 36, 4 << 20, "finish"
    )(meta, idx_row, *parts, hid, gain_row)

    gain_part = jnp.sum(spread(gain_part, AXES, 16, SECOND), axis=0)
    grad_gain = (gain_part + lax.ppermute(gain_part, "c", SWAP)).reshape(width)
    gain_update = grad_gain * lax.rsqrt(jnp.mean(grad_gain * grad_gain) + EPS)
    return (grad_hidden, gain_update)


def solution(mesh):
    fine = Mesh(mesh.devices.reshape(NY, NZL, NC, NX, NZH), AXES)
    dp, mp = ("y", "zl", "c"), ("x", "zh")
    return jax.shard_map(
        body,
        mesh=fine,
        in_specs=(P(dp, mp), P(dp, mp), P(dp, mp), P(dp, mp), P(dp + mp, None), P(), P(dp)),
        out_specs=(P(dp + mp, None), P()),
        check_vma=False,
    )
```

time: 674 us -> 192 us (0.28)
  waiting for transfers between devices: 533 us -> 69 us
  blocking collectives: 97.4 us -> 0 us
  starting transfers between devices: 0.2 us -> 66.4 us
  Pallas kernels: 0 us -> 27.4 us
  matrix products: 13.6 us -> 0 us
    all_gather x4 -> x2, waiting for transfers between devices: 425 us -> 15.6 us  [the longest x1 14.9 us: body(): lax.all_gather(line, AXES, axis=0, tiled=True, axis_index_groups=Y_ON_0)]
    reduce_scatter x1 -> x0, waiting for transfers between devices: 106 us -> none  [body(): lax.psum_scatter(term.astype(jnp.bfloat16), 'mp', scatter_dimension=0, ti...]
    psum x1 -> x0, blocking collectives: 97.4 us -> none  [body(): grad_gain = lax.psum(local_gain, ('dp', 'mp'))]
    ppermute x0 -> x13, starting transfers between devices: none -> 50.1 us  [the longest x3 9.14 us: body(): lax.ppermute(heads, 'x', [(i, (i - d) % NX) for i in range(NX)])]
    ppermute x0 -> x13, waiting for transfers between devices: none -> 28.9 us  [the longest x3 13.3 us: body(): lax.ppermute(heads, 'x', [(i, (i - d) % NX) for i in range(NX)])]
    pallas_call x0 -> x9, Pallas kernels: none -> 27.4 us  [the longest x1 8.38 us: body(): call(backward, [((192, width), BF16), ((192, width), BF16), ((1, width),...]
    all_to_all x0 -> x3, waiting for transfers between devices: none -> 24.4 us  [the longest x1 13.1 us: body(): lines = lax.all_to_all(pair, AXES, 0, 0, axis_index_groups=Z_ON_0)]
    all_to_all x0 -> x3, starting transfers between devices: none -> 16.3 us  [the longest x1 7.14 us: spread(): lax.all_to_all(jnp.broadcast_to(block[None], (size,) + block.shape), axis...]
  transfers between devices with their start and end apart: 5 -> 18, of which waited for: 5 -> 13; matrix products, arithmetic and copies ran while one was open for 1% -> 0% of each run, Pallas kernels for 0% -> 6%
where the time goes in v2:
time: 192 us; the launch traced here: 190 us
  waiting for transfers between devices  69 us (36%)
  starting transfers between devices  66.4 us (35%)
  Pallas kernels  27.4 us (14%)
  between operations  15.2 us (8%)
  local copies, waits for them, and re-layouts  9.63 us (5%)
  other arithmetic  2.81 us (1%)
    all_gather x1, waiting for transfers between devices, body(): lax.all_gather(line, AXES, axis=0, tiled=True, axis_index_groups=Y_ON_0)  14.9 us
    ppermute x3, waiting for transfers between devices, body(): lax.ppermute(heads, 'x', [(i, (i - d) % NX) for i in range(NX)])  13.3 us
    all_to_all x1, waiting for transfers between devices, body(): lines = lax.all_to_all(pair, AXES, 0, 0, axis_index_groups=Z_ON_0)  13.1 us
    ppermute x3, starting transfers between devices, body(): lax.ppermute(heads, 'x', [(i, (i - d) % NX) for i in range(NX)])  9.14 us
    ppermute x1, starting transfers between devices, body(): lax.ppermute(jnp.where(first, w_out, jnp.pad(w_proj, ((0, 8), (0, 0)))),...  8.92 us
    pallas_call x1, Pallas kernels, body(): call(backward, [((192, width), BF16), ((192, width), BF16), ((1, width),...  8.38 us
    ppermute x3, starting transfers between devices, body(): lax.ppermute(parts[d], 'x', [(i, (i + d) % NX) for i in range(NX)])  8.23 us
    all_to_all x1, waiting for transfers between devices, body(): lax.all_to_all(gain_wide, AXES, 0, 0, axis_index_groups=FIRST)  8.04 us
  transfers between devices with their start and end apart: 18, of which 13 were waited for; matrix products, arithmetic and copies ran while one was open for 0% of the time, Pallas kernels for 6%

profile of v2, /device:TPU:1, one launch (start us, length us, event | category | flops | bytes accessed | tf_op | source)
XLA Modules:
  0.0 190.5 jit_solution(6015826873062457733)
XLA Ops:
  7.2 0.0 all-gather.3.cloned.1.call-start
  7.2 0.7 reshape.27.gain.gain_ref
  8.0 0.9 reshape.30.idx
  8.9 0.1 stack.23.meta
  9.0 1.2 copy-done.5
  10.1 1.8 norm.1
  11.9 0.8 copy-done.18
  12.7 0.0 all-gather.3.cloned.1.call-update
  12.8 0.0 copy-start.3
  12.8 0.0 copy-start.4
  12.8 8.9 %collective-permute-start = (bf16[64,512]{1,0:T(8,128)(2,1)S(1)}, bf16[64,512]{1,0:T(8,128)(2,1)S(1)}, u32[]{:S(2)}, u32[]{:S(2)}) collective-permute-start(bf16[64,512]{1,0:T(8,128)(2,1)S(1)} %pad_select_fusion), channel_id=1, source_target_pairs={{0,8},{8,0},{1,9},{9,1},{2,10},{10,2},{3,11},{11,3},{4,12},{12,4},... | collective-permute-start | bytes 196616 | tf_op jit(solution)/shard_map/ppermute | solution.py:246
  21.7 0.9 collective-permute-done.got
  22.6 1.6 pair.1
  24.2 3.6 %all-to-all-start = ((bf16[8,2,64,512]{3,2,1,0:T(8,128)(2,1)}), bf16[8,2,64,512]{3,2,1,0:T(8,128)(2,1)S(1)}, u32[]{:S(2)}, u32[]{:S(2)}) async-start(bf16[8,2,64,512]{3,2,1,0:T(8,128)(2,1)} %pair.1), calls=%async_computation | async-start | bytes 2097152 | tf_op jit(solution)/shard_map/all_to_all | solution.py:250
  27.8 0.0 all-gather.5.cloned.1.call-start
  27.8 3.3 %pick.1 = (bf16[192,1024]{1,0:T(8,128)(2,1)S(1)}, bf16[192,1024]{1,0:T(8,128)(2,1)S(1)}) custom-call(s32[5]{0:T(128)S(1)} %stack.23.meta, s32[8,48,1]{2,1,0:T(8,128)S(1)} %reshape.30.idx, bf16[1024,512]{1,0:T(8,128)(2,1)S(1)} %copy-done.3, bf16[1024,512]{1,0:T(8,128)(2,1)S(1)} %copy-done.4), custom_call_target="tpu_custom_call" | custom-call | flops 100663296 | bytes 3145728 | tf_op jit(solution)/shard_map/pick/pallas_call | solution.py:253
  31.1 0.0 copy-start.6
  31.1 0.7 copy-done.6
  31.9 0.8 copy-done.16
  32.6 13.1 %all-to-all-done.lines = bf16[8,2,64,512]{3,2,1,0:T(8,128)(2,1)S(1)} async-done(((bf16[8,2,64,512]{3,2,1,0:T(8,128)(2,1)}), bf16[8,2,64,512]{3,2,1,0:T(8,128)(2,1)S(1)}, u32[]{:S(2)}, u32[]{:S(2)}) %all-to-all-start) | async-done | bytes 1048608 | tf_op jit(solution)/shard_map/all_to_all | solution.py:250
  45.8 1.6 tighten.1
  47.4 0.7 all-gather.3.cloned.1.call-done.refs_0_
  48.2 0.0 all-gather.5.cloned.1.call-update
  48.2 7.8 %collective-permute-start.1 = (bf16[192,1024]{1,0:T(8,128)(2,1)S(1)}, bf16[192,1024]{1,0:T(8,128)(2,1)S(1)}, u32[]{:S(2)}, u32[]{:S(2)}) collective-permute-start(bf16[192,1024]{1,0:T(8,128)(2,1)S(1)} %copy-done.17), channel_id=1, source_target_pairs={{0,1},{1,0},{2,3},{3,2},{4,5},{5,4},{6,7},{7,6},{8,9},{9,8},{10,11... | collective-permute-start | bytes 1179656 | tf_op jit(solution)/shard_map/ppermute | solution.py:261
  56.0 7.8 %collective-permute-done.1.other = bf16[192,1024]{1,0:T(8,128)(2,1)S(1)} collective-permute-done((bf16[192,1024]{1,0:T(8,128)(2,1)S(1)}, bf16[192,1024]{1,0:T(8,128)(2,1)S(1)}, u32[]{:S(2)}, u32[]{:S(2)}) %collective-permute-start.1) | collective-permute-done | bytes 393248 | tf_op jit(solution)/shard_map/ppermute | solution.py:261
  63.8 0.7 copy-done.13
  64.5 0.6 join.1
  65.1 4.7 %collective-permute-start.2 = (bf16[192,1024]{1,0:T(8,128)(2,1)S(1)}, bf16[192,1024]{1,0:T(8,128)(2,1)S(1)}, u32[]{:S(2)}, u32[]{:S(2)}) collective-permute-start(bf16[192,1024]{1,0:T(8,128)(2,1)S(1)} %get-tuple-element.29.refs_1_), channel_id=1, source_target_pairs={{0,6},{2,0},{4,2},{6,4},{1,7},{3,1},{5,3},{7,5},{8,14},{10,8},{12,... | collective-permute-start | bytes 1179656 | tf_op jit(solution)/shard_map/ppermute | solution.py:264
  69.8 2.3 %collective-permute-start.3 = (bf16[192,1024]{1,0:T(8,128)(2,1)S(1)}, bf16[192,1024]{1,0:T(8,128)(2,1)S(1)}, u32[]{:S(2)}, u32[]{:S(2)}) collective-permute-start(bf16[192,1024]{1,0:T(8,128)(2,1)S(1)} %get-tuple-element.29.refs_1_), channel_id=1, source_target_pairs={{0,4},{2,6},{4,0},{6,2},{1,5},{3,7},{5,1},{7,3},{8,12},{10,14},{12... | collective-permute-start | bytes 1179656 | tf_op jit(solution)/shard_map/ppermute | solution.py:264
  72.1 2.1 %collective-permute-start.4 = (bf16[192,1024]{1,0:T(8,128)(2,1)S(1)}, bf16[192,1024]{1,0:T(8,128)(2,1)S(1)}, u32[]{:S(2)}, u32[]{:S(2)}) collective-permute-start(bf16[192,1024]{1,0:T(8,128)(2,1)S(1)} %get-tuple-element.29.refs_1_), channel_id=1, source_target_pairs={{0,2},{2,4},{4,6},{6,0},{1,3},{3,5},{5,7},{7,1},{8,10},{10,12},{12... | collective-permute-start | bytes 1179656 | tf_op jit(solution)/shard_map/ppermute | solution.py:264
  74.3 5.2 %collective-permute-start.5 = (bf16[192,1024]{1,0:T(8,128)(2,1)S(1)}, bf16[192,1024]{1,0:T(8,128)(2,1)S(1)}, u32[]{:S(2)}, u32[]{:S(2)}) collective-permute-start(bf16[192,1024]{1,0:T(8,128)(2,1)S(1)} %get-tuple-element.32.res_own), channel_id=1, source_target_pairs={{8,0},{10,2},{12,4},{14,6},{24,16},{26,18},{28,20},{30,22},{40,32}... | collective-permute-start | bytes 1179656 | tf_op jit(solution)/shard_map/ppermute | solution.py:262
  79.5 1.8 collective-permute-done.3.refs_3_
  81.4 11.4 %collective-permute-done.4.refs_4_ = bf16[192,1024]{1,0:T(8,128)(2,1)S(1)} collective-permute-done((bf16[192,1024]{1,0:T(8,128)(2,1)S(1)}, bf16[192,1024]{1,0:T(8,128)(2,1)S(1)}, u32[]{:S(2)}, u32[]{:S(2)}) %collective-permute-start.4) | collective-permute-done | bytes 393248 | tf_op jit(solution)/shard_map/ppermute | solution.py:264
  92.8 1.0 choose.1
  93.8 0.0 copy-start.8
  93.8 0.8 copy-done.8
  94.6 2.3 %collective-permute-start.6 = (bf16[192,4096]{1,0:T(8,128)(2,1)S(1)}, bf16[192,4096]{1,0:T(8,128)(2,1)S(1)}, u32[]{:S(2)}, u32[]{:S(2)}) collective-permute-start(bf16[192,4096]{1,0:T(8,128)(2,1)S(1)} %get-tuple-element.33), channel_id=1, source_target_pairs={{0,8},{8,0},{1,9},{9,1},{2,10},{10,2},{3,11},{11,3},{4,12},{12,4},... | collective-permute-start | bytes 4718600 | tf_op jit(solution)/shard_map/ppermute | solution.py:269
  96.9 3.0 %collective-permute-done.6.oth = bf16[192,4096]{1,0:T(8,128)(2,1)S(1)} collective-permute-done((bf16[192,4096]{1,0:T(8,128)(2,1)S(1)}, bf16[192,4096]{1,0:T(8,128)(2,1)S(1)}, u32[]{:S(2)}, u32[]{:S(2)}) %collective-permute-start.6) | collective-permute-done | bytes 1572896 | tf_op jit(solution)/shard_map/ppermute | solution.py:269
  99.9 14.9 %all-gather.5.cloned.1.call-done = bf16[8192,512]{1,0:T(8,128)(2,1)} async-done(((bf16[1024,512]{1,0:T(8,128)(2,1)}), bf16[8192,512]{1,0:T(8,128)(2,1)}) %all-gather.5.cloned.1.call-update) | async-done | bytes 8388624 | tf_op jit(solution)/shard_map/all_gather | solution.py:257
  114.8 0.7 copy-done.14
  115.5 6.6 %forward.1 = (f32[384,1024]{1,0:T(8,128)S(1)}, bf16[384,1024]{1,0:T(8,128)(2,1)S(1)}) custom-call(s32[5]{0:T(128)S(1)} %copy-done.14, bf16[192,4096]{1,0:T(8,128)(2,1)S(1)} %get-tuple-element.30.own, bf16[192,4096]{1,0:T(8,128)(2,1)S(1)} %collective-permute-done.6.oth, bf16[8,1024,512]{2,1,0:T(8,128)(2,1)} %bitcast.18), custom_call_target="tpu_custom_call" | custom-call | flops 3221225472 | bytes 13631488 | tf_op jit(solution)/shard_map/forward/pallas_call | solution.py:272
  122.0 1.5 collective-permute-start.7
  123.6 1.7 collective-permute-done.7.teach
  125.2 8.4 %backward.1 = (bf16[192,3584]{1,0:T(8,128)(2,1)S(1)}, bf16[192,3584]{1,0:T(8,128)(2,1)S(1)}, f32[1,3584]{1,0:T(1,128)S(1)}) custom-call(s32[5]{0:T(128)S(1)} %copy-done.14, f32[384,1024]{1,0:T(8,128)S(1)} %get-tuple-element.35.pred, bf16[384,1024]{1,0:T(8,128)(2,1)S(1)} %collective-permute-done.7.teach, bf16[192,1024]{1,0:T(8,128)(2,1)S(1)} %get-tuple-element.32.res_own, ...), custom_call_target="tpu_custom_call" | custom-call | flops 2818572288 | bytes 16777216 | tf_op jit(solution)/shard_map/backward/pallas_call | solution.py:282
  133.7 0.7 broadcast_in_dim.14
  134.4 1.3 collective-permute-start.8
  135.7 5.6 %all-to-all-start.1 = ((f32[16,28,128]{2,1,0:T(8,128)}), f32[16,28,128]{2,1,0:T(8,128)S(1)}, u32[]{:S(2)}, u32[]{:S(2)}) async-start(f32[16,28,128]{2,1,0:T(8,128)} %broadcast_in_dim.14), calls=%async_computation.1 | async-start | bytes 524288 | tf_op jit(solution)/shard_map/all_to_all | solution.py:294
  141.3 8.0 %all-to-all-done.1 = f32[16,28,128]{2,1,0:T(8,128)S(1)} async-done(((f32[16,28,128]{2,1,0:T(8,128)}), f32[16,28,128]{2,1,0:T(8,128)S(1)}, u32[]{:S(2)}, u32[]{:S(2)}) %all-to-all-start.1) | async-done | bytes 229408 | tf_op jit(solution)/shard_map/all_to_all | solution.py:294
  149.4 1.5 broadcast_select_fusion
  150.9 0.0 copy-start.20
  150.9 0.0 copy-start.15
  150.9 0.8 dynamic-slice_bitcast_fusion
  151.8 0.7 broadcast_in_dim.15
  152.5 7.1 %all-to-all-start.2 = ((f32[16,28,128]{2,1,0:T(8,128)}), f32[16,28,128]{2,1,0:T(8,128)S(1)}, u32[]{:S(2)}, u32[]{:S(2)}) async-start(f32[16,28,128]{2,1,0:T(8,128)} %broadcast_in_dim.15), calls=%async_computation.2 | async-start | bytes 524288 | tf_op jit(solution)/shard_map/all_to_all | solution.py:219
  159.6 2.9 %collective-permute-start.10 = (bf16[48,3584]{1,0:T(8,128)(2,1)}, bf16[48,3584]{1,0:T(8,128)(2,1)S(1)}, u32[]{:S(2)}, u32[]{:S(2)}) collective-permute-start(bf16[48,3584]{1,0:T(8,128)(2,1)} %get-tuple-element.49), channel_id=1, source_target_pairs={{0,4},{2,6},{4,0},{6,2},{1,5},{3,7},{5,1},{7,3},{8,12},{10,14},{12... | collective-permute-start | bytes 1032200 | tf_op jit(solution)/shard_map/ppermute | solution.py:301
  162.6 3.3 %collective-permute-start.11 = (bf16[48,3584]{1,0:T(8,128)(2,1)S(1)}, bf16[48,3584]{1,0:T(8,128)(2,1)S(1)}, u32[]{:S(2)}, u32[]{:S(2)}) collective-permute-start(bf16[48,3584]{1,0:T(8,128)(2,1)S(1)} %get-tuple-element.48), channel_id=1, source_target_pairs={{0,6},{2,0},{4,2},{6,4},{1,7},{3,1},{5,3},{7,5},{8,14},{10,8},{12,... | collective-permute-start | bytes 1032200 | tf_op jit(solution)/shard_map/ppermute | solution.py:301
  165.8 2.0 %collective-permute-start.9 = (bf16[48,3584]{1,0:T(8,128)(2,1)S(1)}, bf16[48,3584]{1,0:T(8,128)(2,1)S(1)}, u32[]{:S(2)}, u32[]{:S(2)}) collective-permute-start(bf16[48,3584]{1,0:T(8,128)(2,1)S(1)} %get-tuple-element.50), channel_id=1, source_target_pairs={{0,2},{2,4},{4,6},{6,0},{1,3},{3,5},{5,7},{7,1},{8,10},{10,12},{12... | collective-permute-start | bytes 1032200 | tf_op jit(solution)/shard_map/ppermute | solution.py:301
  167.9 3.3 %all-to-all-done.2 = f32[16,28,128]{2,1,0:T(8,128)S(1)} async-done(((f32[16,28,128]{2,1,0:T(8,128)}), f32[16,28,128]{2,1,0:T(8,128)S(1)}, u32[]{:S(2)}, u32[]{:S(2)}) %all-to-all-start.2) | async-done | bytes 229408 | tf_op jit(solution)/shard_map/all_to_all | solution.py:219
  171.2 5.7 %collective-permute-start.12 = (f32[28,128]{1,0:T(8,128)S(1)}, f32[28,128]{1,0:T(8,128)S(1)}, u32[]{:S(2)}, u32[]{:S(2)}) collective-permute-start(f32[28,128]{1,0:T(8,128)S(1)} %reduce_sum.28), channel_id=1, source_target_pairs={{0,8},{8,0},{1,9},{9,1},{2,10},{10,2},{3,11},{11,3},{4,12},{12,4},... | collective-permute-start | bytes 43016 | tf_op jit(solution)/shard_map/ppermute | solution.py:307
  176.9 0.1 collective-permute-done.11.part3
  176.9 2.2 %collective-permute-done.9.part1 = bf16[48,3584]{1,0:T(8,128)(2,1)S(1)} collective-permute-done((bf16[48,3584]{1,0:T(8,128)(2,1)S(1)}, bf16[48,3584]{1,0:T(8,128)(2,1)S(1)}, u32[]{:S(2)}, u32[]{:S(2)}) %collective-permute-start.9) | collective-permute-done | bytes 344096 | tf_op jit(solution)/shard_map/ppermute | solution.py:301
  179.1 2.6 %finish.1 = bf16[128,3584]{1,0:T(8,128)(2,1)} custom-call(s32[5]{0:T(128)S(1)} %copy-done.15, s32[1,384]{1,0:T(1,128)S(1)} %reshape.25.idx, bf16[48,3584]{1,0:T(8,128)(2,1)S(1)} %get-tuple-element.43.part0, bf16[48,3584]{1,0:T(8,128)(2,1)S(1)} %collective-permute-done.9.part1, bf16[48,3584]{1,0:T(8,128)(2,1)S(1)} %collective-permute-done.10.part2, ...), custom_call_target="tpu_custom_call" | custom-call | flops 68719476736 | bytes 4194304 | tf_op jit(solution)/shard_map/finish/pallas_call | solution.py:302
  181.7 0.6 multiply_reduce_fusion
  183.0 0.6 multiply_bitcast_fusion
  (39 shorter events, 0.2 us)
Async XLA Ops:
  7.2 5.6 %copy-start.11 = (bf16[56,512]{1,0:T(8,128)(2,1)S(1)}, bf16[56,512]{1,0:T(8,128)(2,1)}, u32[]{:S(2)}) copy-start(bf16[56,512]{1,0:T(8,128)(2,1)} %proj.1) | copy-start | bytes 172036
  7.2 5.6 %copy-start.10 = (bf16[64,512]{1,0:T(8,128)(2,1)S(1)}, bf16[64,512]{1,0:T(8,128)(2,1)}, u32[]{:S(2)}) copy-start(bf16[64,512]{1,0:T(8,128)(2,1)} %outp.1) | copy-start | bytes 196612
  7.2 41.0 %all-gather.3.cloned.1.call-start = ((), (), s32[]{:S(2)}) async-start(), calls=%async_computation.3 | async-start | bytes 1720320 | tf_op jit(solution)/shard_map/all_gather | solution.py:244
  9.0 1.2 copy-start.5
  10.1 35.7 %copy-start.12 = (s32[5]{0:T(128)}, s32[5]{0:T(128)S(1)}, u32[]{:S(2)}) copy-start(s32[5]{0:T(128)S(1)} %stack.23.meta) | copy-start | bytes 64
  11.9 0.8 copy-start.18
  12.8 15.1 %copy-start.3 = (bf16[1024,512]{1,0:T(8,128)(2,1)S(1)}, bf16[1024,512]{1,0:T(8,128)(2,1)}, u32[]{:S(2)}) copy-start(bf16[1024,512]{1,0:T(8,128)(2,1)} %context.1) | copy-start | bytes 3145732
  12.8 15.1 %copy-start.4 = (bf16[1024,512]{1,0:T(8,128)(2,1)S(1)}, bf16[1024,512]{1,0:T(8,128)(2,1)}, u32[]{:S(2)}) copy-start(bf16[1024,512]{1,0:T(8,128)(2,1)} %residual.1) | copy-start | bytes 3145732
  12.8 9.8 %collective-permute-start = (bf16[64,512]{1,0:T(8,128)(2,1)S(1)}, bf16[64,512]{1,0:T(8,128)(2,1)S(1)}, u32[]{:S(2)}, u32[]{:S(2)}) collective-permute-start(bf16[64,512]{1,0:T(8,128)(2,1)S(1)} %pad_select_fusion), channel_id=1, source_target_pairs={{0,8},{8,0},{1,9},{9,1},{2,10},{10,2},{3,11},{11,3},{4,12},{12,4},... | collective-permute-start | bytes 196616 | tf_op jit(solution)/shard_map/ppermute | solution.py:246
  24.2 21.6 %all-to-all-start = ((bf16[8,2,64,512]{3,2,1,0:T(8,128)(2,1)}), bf16[8,2,64,512]{3,2,1,0:T(8,128)(2,1)S(1)}, u32[]{:S(2)}, u32[]{:S(2)}) async-start(bf16[8,2,64,512]{3,2,1,0:T(8,128)(2,1)} %pair.1), calls=%async_computation | async-start | bytes 2097152 | tf_op jit(solution)/shard_map/all_to_all | solution.py:250
  27.8 87.0 %all-gather.5.cloned.1.call-start = ((), (), s32[]{:S(2)}) async-start(), calls=%async_computation.4 | async-start | bytes 9437184 | tf_op jit(solution)/shard_map/all_gather | solution.py:257
  31.1 0.7 copy-start.6
  31.9 0.8 copy-start.16
  45.8 2.4 %copy-start.17 = (bf16[192,1024]{1,0:T(8,128)(2,1)S(1)}, bf16[192,1024]{1,0:T(8,128)(2,1)}, u32[]{:S(2)}) copy-start(bf16[192,1024]{1,0:T(8,128)(2,1)} %copy-done.16) | copy-start | bytes 1179652
  45.8 18.0 %copy-start.7 = (bf16[192,1024]{1,0:T(8,128)(2,1)S(1)}, bf16[192,1024]{1,0:T(8,128)(2,1)}, u32[]{:S(2)}) copy-start(bf16[192,1024]{1,0:T(8,128)(2,1)} %copy-done.6) | copy-start | bytes 1179652
  48.2 44.6 %copy-start.2 = (bf16[192,3584]{1,0:T(8,128)(2,1)S(1)}, bf16[192,3584]{1,0:T(8,128)(2,1)}, u32[]{:S(2)}) copy-start(bf16[192,3584]{1,0:T(8,128)(2,1)} %all-gather.3.cloned.1.call-done.refs_0_) | copy-start | bytes 4128772
  48.2 15.6 %collective-permute-start.1 = (bf16[192,1024]{1,0:T(8,128)(2,1)S(1)}, bf16[192,1024]{1,0:T(8,128)(2,1)S(1)}, u32[]{:S(2)}, u32[]{:S(2)}) collective-permute-start(bf16[192,1024]{1,0:T(8,128)(2,1)S(1)} %copy-done.17), channel_id=1, source_target_pairs={{0,1},{1,0},{2,3},{3,2},{4,5},{5,4},{6,7},{7,6},{8,9},{9,8},{10,11... | collective-permute-start | bytes 1179656 | tf_op jit(solution)/shard_map/ppermute | solution.py:261
  63.8 0.7 copy-start.13
  65.1 14.4 %collective-permute-start.2 = (bf16[192,1024]{1,0:T(8,128)(2,1)S(1)}, bf16[192,1024]{1,0:T(8,128)(2,1)S(1)}, u32[]{:S(2)}, u32[]{:S(2)}) collective-permute-start(bf16[192,1024]{1,0:T(8,128)(2,1)S(1)} %get-tuple-element.29.refs_1_), channel_id=1, source_target_pairs={{0,6},{2,0},{4,2},{6,4},{1,7},{3,1},{5,3},{7,5},{8,14},{10,8},{12,... | collective-permute-start | bytes 1179656 | tf_op jit(solution)/shard_map/ppermute | solution.py:264
  69.8 11.5 %collective-permute-start.3 = (bf16[192,1024]{1,0:T(8,128)(2,1)S(1)}, bf16[192,1024]{1,0:T(8,128)(2,1)S(1)}, u32[]{:S(2)}, u32[]{:S(2)}) collective-permute-start(bf16[192,1024]{1,0:T(8,128)(2,1)S(1)} %get-tuple-element.29.refs_1_), channel_id=1, source_target_pairs={{0,4},{2,6},{4,0},{6,2},{1,5},{3,7},{5,1},{7,3},{8,12},{10,14},{12... | collective-permute-start | bytes 1179656 | tf_op jit(solution)/shard_map/ppermute | solution.py:264
  72.1 20.7 %collective-permute-start.4 = (bf16[192,1024]{1,0:T(8,128)(2,1)S(1)}, bf16[192,1024]{1,0:T(8,128)(2,1)S(1)}, u32[]{:S(2)}, u32[]{:S(2)}) collective-permute-start(bf16[192,1024]{1,0:T(8,128)(2,1)S(1)} %get-tuple-element.29.refs_1_), channel_id=1, source_target_pairs={{0,2},{2,4},{4,6},{6,0},{1,3},{3,5},{5,7},{7,1},{8,10},{10,12},{12... | collective-permute-start | bytes 1179656 | tf_op jit(solution)/shard_map/ppermute | solution.py:264
  74.3 19.5 %collective-permute-start.5 = (bf16[192,1024]{1,0:T(8,128)(2,1)S(1)}, bf16[192,1024]{1,0:T(8,128)(2,1)S(1)}, u32[]{:S(2)}, u32[]{:S(2)}) collective-permute-start(bf16[192,1024]{1,0:T(8,128)(2,1)S(1)} %get-tuple-element.32.res_own), channel_id=1, source_target_pairs={{8,0},{10,2},{12,4},{14,6},{24,16},{26,18},{28,20},{30,22},{40,32}... | collective-permute-start | bytes 1179656 | tf_op jit(solution)/shard_map/ppermute | solution.py:262
  93.8 28.2 %copy-start = (bf16[192,4096]{1,0:T(8,128)(2,1)}, bf16[192,4096]{1,0:T(8,128)(2,1)S(1)}, u32[]{:S(2)}) copy-start(bf16[192,4096]{1,0:T(8,128)(2,1)S(1)} %get-tuple-element.30.own) | copy-start | bytes 4718596
  93.8 0.8 copy-start.8
  94.6 5.3 %collective-permute-start.6 = (bf16[192,4096]{1,0:T(8,128)(2,1)S(1)}, bf16[192,4096]{1,0:T(8,128)(2,1)S(1)}, u32[]{:S(2)}, u32[]{:S(2)}) collective-permute-start(bf16[192,4096]{1,0:T(8,128)(2,1)S(1)} %get-tuple-element.33), channel_id=1, source_target_pairs={{0,8},{8,0},{1,9},{9,1},{2,10},{10,2},{3,11},{11,3},{4,12},{12,4},... | collective-permute-start | bytes 4718600 | tf_op jit(solution)/shard_map/ppermute | solution.py:269
  99.9 22.1 %copy-start.1 = (bf16[192,4096]{1,0:T(8,128)(2,1)}, bf16[192,4096]{1,0:T(8,128)(2,1)S(1)}, u32[]{:S(2)}) copy-start(bf16[192,4096]{1,0:T(8,128)(2,1)S(1)} %collective-permute-done.6.oth) | copy-start | bytes 4718596
  114.8 0.7 copy-start.14
  115.5 9.8 %copy-start.9 = (bf16[192,1024]{1,0:T(8,128)(2,1)S(1)}, bf16[192,1024]{1,0:T(8,128)(2,1)}, u32[]{:S(2)}) copy-start(bf16[192,1024]{1,0:T(8,128)(2,1)} %copy-done.8) | copy-start | bytes 1179652
  122.0 3.2 %collective-permute-start.7 = (bf16[384,1024]{1,0:T(8,128)(2,1)S(1)}, bf16[384,1024]{1,0:T(8,128)(2,1)S(1)}, u32[]{:S(2)}, u32[]{:S(2)}) collective-permute-start(bf16[384,1024]{1,0:T(8,128)(2,1)S(1)} %get-tuple-element.36), channel_id=1, source_target_pairs={{8,0},{10,2},{12,4},{14,6},{24,16},{26,18},{28,20},{30,22},{40,32}... | collective-permute-start | bytes 2359304 | tf_op jit(solution)/shard_map/ppermute | solution.py:281
  134.4 15.0 %collective-permute-start.8 = (bf16[192,3584]{1,0:T(8,128)(2,1)S(1)}, bf16[192,3584]{1,0:T(8,128)(2,1)}, u32[]{:S(2)}, u32[]{:S(2)}) collective-permute-start(bf16[192,3584]{1,0:T(8,128)(2,1)S(1)} %get-tuple-element.42), channel_id=1, source_target_pairs={{0,8},{2,10},{4,12},{6,14},{16,24},{18,26},{20,28},{22,30},{32,40}... | collective-permute-start | bytes 4128776 | tf_op jit(solution)/shard_map/ppermute | solution.py:296
  135.7 13.7 %all-to-all-start.1 = ((f32[16,28,128]{2,1,0:T(8,128)}), f32[16,28,128]{2,1,0:T(8,128)S(1)}, u32[]{:S(2)}, u32[]{:S(2)}) async-start(f32[16,28,128]{2,1,0:T(8,128)} %broadcast_in_dim.14), calls=%async_computation.1 | async-start | bytes 524288 | tf_op jit(solution)/shard_map/all_to_all | solution.py:294
  150.9 17.0 %copy-start.20 = (s32[384]{0:T(512)S(1)}, s32[384]{0:T(512)}, u32[]{:S(2)}) copy-start(s32[384]{0:T(512)} %param.13) | copy-start | bytes 4612
  150.9 28.2 %copy-start.15 = (s32[5]{0:T(128)S(1)}, s32[5]{0:T(128)}, u32[]{:S(2)}) copy-start(s32[5]{0:T(128)} %copy-done.12) | copy-start | bytes 64
  150.9 28.2 %copy-start.19 = (bf16[48,3584]{1,0:T(8,128)(2,1)S(1)}, bf16[48,3584]{1,0:T(8,128)(2,1)}, u32[]{:S(2)}) copy-start(bf16[48,3584]{1,0:T(8,128)(2,1)} %copy-done.18) | copy-start | bytes 1032196
  152.5 18.7 %all-to-all-start.2 = ((f32[16,28,128]{2,1,0:T(8,128)}), f32[16,28,128]{2,1,0:T(8,128)S(1)}, u32[]{:S(2)}, u32[]{:S(2)}) async-start(f32[16,28,128]{2,1,0:T(8,128)} %broadcast_in_dim.15), calls=%async_computation.2 | async-start | bytes 524288 | tf_op jit(solution)/shard_map/all_to_all | solution.py:219
  159.6 17.2 %collective-permute-start.10 = (bf16[48,3584]{1,0:T(8,128)(2,1)}, bf16[48,3584]{1,0:T(8,128)(2,1)S(1)}, u32[]{:S(2)}, u32[]{:S(2)}) collective-permute-start(bf16[48,3584]{1,0:T(8,128)(2,1)} %get-tuple-element.49), channel_id=1, source_target_pairs={{0,4},{2,6},{4,0},{6,2},{1,5},{3,7},{5,1},{7,3},{8,12},{10,14},{12... | collective-permute-start | bytes 1032200 | tf_op jit(solution)/shard_map/ppermute | solution.py:301
  162.6 14.3 %collective-permute-start.11 = (bf16[48,3584]{1,0:T(8,128)(2,1)S(1)}, bf16[48,3584]{1,0:T(8,128)(2,1)S(1)}, u32[]{:S(2)}, u32[]{:S(2)}) collective-permute-start(bf16[48,3584]{1,0:T(8,128)(2,1)S(1)} %get-tuple-element.48), channel_id=1, source_target_pairs={{0,6},{2,0},{4,2},{6,4},{1,7},{3,1},{5,3},{7,5},{8,14},{10,8},{12,... | collective-permute-start | bytes 1032200 | tf_op jit(solution)/shard_map/ppermute | solution.py:301
  165.8 13.3 %collective-permute-start.9 = (bf16[48,3584]{1,0:T(8,128)(2,1)S(1)}, bf16[48,3584]{1,0:T(8,128)(2,1)S(1)}, u32[]{:S(2)}, u32[]{:S(2)}) collective-permute-start(bf16[48,3584]{1,0:T(8,128)(2,1)S(1)} %get-tuple-element.50), channel_id=1, source_target_pairs={{0,2},{2,4},{4,6},{6,0},{1,3},{3,5},{5,7},{7,1},{8,10},{10,12},{12... | collective-permute-start | bytes 1032200 | tf_op jit(solution)/shard_map/ppermute | solution.py:301
  171.2 10.5 %collective-permute-start.12 = (f32[28,128]{1,0:T(8,128)S(1)}, f32[28,128]{1,0:T(8,128)S(1)}, u32[]{:S(2)}, u32[]{:S(2)}) collective-permute-start(f32[28,128]{1,0:T(8,128)S(1)} %reduce_sum.28), channel_id=1, source_target_pairs={{0,8},{8,0},{1,9},{9,1},{2,10},{10,2},{3,11},{11,3},{4,12},{12,4},... | collective-permute-start | bytes 43016 | tf_op jit(solution)/shard_map/ppermute | solution.py:307
Sparse Core Ops, SparseCore 0:
  12.8 35.2 all-gather.2
  50.2 64.5 all-gather.4

commit v3 on v2

--- a/solution.py
+++ b/solution.py
@@ -39,6 +39,8 @@
     for y in range(4)
 ]
 SWAP = [(0, 1), (1, 0)]
+DOWN = [(dev(y, z, 0, x), dev(y, z, 1, x)) for y, z, x in CHIPS]
+UP = [(b, a) for a, b in DOWN]
 
 VMEM = pl.BlockSpec(memory_space=pltpu.VMEM)
 SMEM = pl.BlockSpec(memory_space=pltpu.SMEM)
@@ -129,16 +131,18 @@
 
 
 def choose(meta, *refs):
-    normed, heads, (keep, give) = refs[0], refs[1 : 1 + NX], refs[1 + NX :]
+    normed, heads, (keep, give) = refs[:NX], refs[NX : 2 * NX], refs[2 * NX :]
 
     def put(core, to_normed, to_heads):
         @pl.when(meta[3] == core)
         def _():
             for y in range(NY):
-                to_normed[:, y * 512 : y * 512 + 448] = normed[:, y * 448 : y * 448 + 448]
                 to_normed[:, y * 512 + 448 : y * 512 + 512] = jnp.zeros((192, 64), BF16)
             for d in range(NX):
                 x = (meta[4] + d) % NX
+                rows = pl.ds(pl.multiple_of(x * 48, 16), 48)
+                for y in range(NY):
+                    to_normed[rows, y * 512 : y * 512 + 448] = normed[d][:, y * 448 : y * 448 + 448]
                 to_heads[:, pl.ds(pl.multiple_of(x * 1024, 1024), 1024)] = heads[d][...]
 
     put(0, keep, give)
@@ -191,18 +195,16 @@
         term = lax.dot_general(g_buf[:, :512], buf[y, :448, :], NT, preferred_element_type=F32)
         term = term + lax.dot_general(g_buf[:, 512:], buf[y, 512:960, :], NT, preferred_element_type=F32)
         a = jnp.concatenate([own[:, lanes], oth[:, lanes]], axis=0).astype(F32)
-        total = jnp.sum(term * a, axis=0, keepdims=True) / gain[:, cols]
-        gain_out[:, cols] = jnp.where(meta[3] == 0, total, 0.0)
+        gain_out[:, cols] = jnp.sum(term * a, axis=0, keepdims=True) / gain[:, cols]
         term = term.astype(BF16)
         term_own[:, cols] = term[:192]
         term_oth[:, cols] = term[192:]
 
 
-def finish(meta, idx, part0, part1, part2, part3, hid_ref, gain_ref, out):
+def finish(meta, idx, summed, hid_ref, gain_ref, out):
     gain = gain_ref[...]
     hid = hid_ref[...].astype(F32)
-    scaled = (part0[...].astype(F32) + part1[...].astype(F32)) + (part2[...].astype(F32) + part3[...].astype(F32))
-    scaled = scaled * gain
+    scaled = summed[...].astype(F32) * gain
     width = hid.shape[1]
     stat = lax.rsqrt(jnp.mean(hid * hid, axis=1, keepdims=True) + EPS)
     inner = jnp.sum(hid * scaled, axis=1, keepdims=True)
@@ -241,7 +243,6 @@
         2 << 20,
         "norm",
     )(meta, idx, hidden, gain_row)
-    normed = lax.all_gather(normed, "x", axis=0, tiled=True)
 
     got = lax.ppermute(jnp.where(first, w_out, jnp.pad(w_proj, ((0, 8), (0, 0)))), "c", SWAP)
     (pair,) = call(
@@ -256,15 +257,20 @@
     line, away, normed = lax.optimization_barrier((line, away, normed))
     w = lax.all_gather(line, AXES, axis=0, tiled=True, axis_index_groups=Y_ON_0).reshape(8, 1024, 512)
 
+    other = lax.ppermute(away, "zh", SWAP)
+
+    def around(block):
+        return [block] + [lax.ppermute(block, "x", [(i, (i - d) % NX) for i in range(NX)]) for d in range(1, NX)]
+
+    normed = around(normed)
     heads, res_own = call(
         join, [((192, 1024), BF16)] * 2, [SMEM, VMEM, VMEM], [], 0, 3 << 20, "join"
-    )(meta, here, lax.ppermute(away, "zh", SWAP))
-    res_oth = lax.ppermute(res_own, AXES, [(dev(y, z, 1, x), dev(y, z, 0, x)) for y, z, x in CHIPS])
-
-    heads = [heads] + [lax.ppermute(heads, "x", [(i, (i - d) % NX) for i in range(NX)]) for d in range(1, NX)]
+    )(meta, here, other)
+    res_oth = lax.ppermute(res_own, AXES, UP)
+
     keep, give = call(
-        choose, [((192, 4096), BF16)] * 2, [SMEM] + [VMEM] * 5, [], 0, 6 << 20, "choose"
-    )(meta, normed, *heads)
+        choose, [((192, 4096), BF16)] * 2, [SMEM] + [VMEM] * 8, [], 0, 6 << 20, "choose"
+    )(meta, *normed, *around(heads))
     give, res_oth = lax.optimization_barrier((give, res_oth))
     taken = lax.ppermute(give, "c", SWAP)
 
@@ -278,7 +284,7 @@
         13 << 20,
         "forward",
     )(meta, keep, taken, w)
-    teach = lax.ppermute(teach, AXES, [(dev(y, z, 1, x), dev(y, z, 0, x)) for y, z, x in CHIPS])
+    teach = lax.ppermute(teach, AXES, UP)
     term_own, term_oth, gain_part = call(
         backward,
         [((192, width), BF16), ((192, width), BF16), ((1, width), F32)],
@@ -289,22 +295,19 @@
         "backward",
     )(meta, pred, teach, res_own, res_oth, keep, taken, gain_row, w)
 
-    gain_wide = jnp.broadcast_to(gain_part.reshape(1, 28, 128), (16, 28, 128))
-    gain_wide, term_oth = lax.optimization_barrier((gain_wide, term_oth))
+    gain_part = gain_part.reshape(28, 128)
+    gain_part = jnp.where(first, gain_part, lax.ppermute(gain_part, AXES, DOWN))
+    gain_wide = jnp.broadcast_to(gain_part[None], (16, 28, 128))
+    gain_wide, handed = lax.optimization_barrier((gain_wide, lax.ppermute(term_oth, AXES, DOWN)))
     gain_part = jnp.sum(lax.all_to_all(gain_wide, AXES, 0, 0, axis_index_groups=FIRST), axis=0)
 
-    handed = lax.ppermute(term_oth, AXES, [(dev(y, z, 0, x), dev(y, z, 1, x)) for y, z, x in CHIPS])
-    summed = jnp.where(first, term_own, handed).reshape(NX, 48, width)
-    parts = [lax.dynamic_index_in_dim(summed, (x + d) % NX, 0, keepdims=False) for d in range(NX)]
-    gain_part, parts[0] = lax.optimization_barrier((gain_part, parts[0]))
-    for d in range(1, NX):
-        parts[d] = lax.ppermute(parts[d], "x", [(i, (i + d) % NX) for i in range(NX)])
+    summed = lax.psum_scatter(jnp.where(first, term_own, handed), "x", scatter_dimension=0, tiled=True)
     (grad_hidden,) = call(
-        finish, [((own_rows, width), BF16)], [SMEM] + [VMEM] * 7, [], 1 << 36, 4 << 20, "finish"
-    )(meta, idx_row, *parts, hid, gain_row)
-
-    gain_part = jnp.sum(spread(gain_part, AXES, 16, SECOND), axis=0)
-    grad_gain = (gain_part + lax.ppermute(gain_part, "c", SWAP)).reshape(width)
+        finish, [((own_rows, width), BF16)], [SMEM] + [VMEM] * 4, [], 2 * 128 * 48 * width, 4 << 20, "finish"
+    )(meta, idx_row, summed, hid, gain_row)
+
+    gathered, grad_hidden = lax.optimization_barrier((spread(gain_part, AXES, 16, SECOND), grad_hidden))
+    grad_gain = jnp.sum(gathered, axis=0).reshape(width)
     gain_update = grad_gain * lax.rsqrt(jnp.mean(grad_gain * grad_gain) + EPS)
     return (grad_hidden, gain_update)
 

time: 192 us -> 190 us (0.990)
  waiting for transfers between devices: 69 us -> 50 us
  blocking collectives: 0 us -> 14.9 us
  other arithmetic: 2.81 us -> 4.76 us
    all_to_all x0 -> x1, blocking collectives: none -> 14.9 us  [body(): lax.all_to_all(gain_wide, AXES, 0, 0, axis_index_groups=FIRST)]
    all_gather x1, waiting for transfers between devices: 14.9 us -> 0.16 us  [body(): lax.all_gather(line, AXES, axis=0, tiled=True, axis_index_groups=Y_ON_0)]
    all_to_all x1 -> x0, waiting for transfers between devices: 8.04 us -> none  [body(): lax.all_to_all(gain_wide, AXES, 0, 0, axis_index_groups=FIRST)]
    all_to_all x1, starting transfers between devices: 7.14 us -> 13.9 us  [spread(): lax.all_to_all(jnp.broadcast_to(block[None], (size,) + block.shape), axis...]
    all_to_all x1 -> x0, starting transfers between devices: 5.56 us -> none  [body(): lax.all_to_all(gain_wide, AXES, 0, 0, axis_index_groups=FIRST)]
    all_to_all x1, waiting for transfers between devices: 3.26 us -> 7.85 us  [spread(): lax.all_to_all(jnp.broadcast_to(block[None], (size,) + block.shape), axis...]
    all_to_all x1, waiting for transfers between devices: 13.1 us -> 9.2 us  [body(): lines = lax.all_to_all(pair, AXES, 0, 0, axis_index_groups=Z_ON_0)]
    unnamed x42 -> x50, local copies, waits for them, and re-layouts: 5.63 us -> 9.03 us
  transfers between devices with their start and end apart: 18 -> 17, of which waited for: 13 -> 10; matrix products, arithmetic and copies ran while one was open for 0% -> 1% of each run, Pallas kernels for 6% -> 4%
where the time goes in v3:
time: 190 us; the launch traced here: 187 us
  starting transfers between devices  66.2 us (35%)
  waiting for transfers between devices  50 us (26%)
  Pallas kernels  26.4 us (14%)
  between operations  15.1 us (8%)
  blocking collectives  14.9 us (8%)
  local copies, waits for them, and re-layouts  10.1 us (5%)
  other arithmetic  4.76 us (3%)
    ppermute x6, starting transfers between devices, around(): lax.ppermute(block, 'x', [(i, (i - d) % NX) for i in range(NX)])  19.2 us
    ppermute x6, waiting for transfers between devices, around(): lax.ppermute(block, 'x', [(i, (i - d) % NX) for i in range(NX)])  17 us
    all_to_all x1, blocking collectives, body(): lax.all_to_all(gain_wide, AXES, 0, 0, axis_index_groups=FIRST)  14.9 us
    all_to_all x1, starting transfers between devices, spread(): lax.all_to_all(jnp.broadcast_to(block[None], (size,) + block.shape), axis...  13.9 us
    all_to_all x1, waiting for transfers between devices, body(): lines = lax.all_to_all(pair, AXES, 0, 0, axis_index_groups=Z_ON_0)  9.2 us
    unnamed x50, local copies, waits for them, and re-layouts  9.03 us
    ppermute x1, starting transfers between devices, body(): lax.ppermute(jnp.where(first, w_out, jnp.pad(w_proj, ((0, 8), (0, 0)))),...  8.82 us
    pallas_call x1, Pallas kernels, body(): call(backward, [((192, width), BF16), ((192, width), BF16), ((1, width),...  8.37 us
  transfers between devices with their start and end apart: 17, of which 10 were waited for; matrix products, arithmetic and copies ran while one was open for 1% of the time, Pallas kernels for 4%

profile of v3, /device:TPU:1, one launch (start us, length us, event | category | flops | bytes accessed | tf_op | source)
XLA Modules:
  0.0 187.5 jit_solution(4041290803499008479)
XLA Ops:
  7.2 0.8 pad_select_fusion
  8.0 8.8 %collective-permute-start = (bf16[64,512]{1,0:T(8,128)(2,1)S(1)}, bf16[64,512]{1,0:T(8,128)(2,1)S(1)}, u32[]{:S(2)}, u32[]{:S(2)}) collective-permute-start(bf16[64,512]{1,0:T(8,128)(2,1)S(1)} %pad_select_fusion), channel_id=1, source_target_pairs={{0,8},{8,0},{1,9},{9,1},{2,10},{10,2},{3,11},{11,3},{4,12},{12,4},... | collective-permute-start | bytes 196616 | tf_op jit(solution)/shard_map/ppermute | solution.py:247
  16.9 0.1 stack.23.meta
  16.9 0.8 collective-permute-done.got
  17.7 0.8 copy-done.14
  18.6 0.8 copy-done.15
  19.4 1.6 pair.1
  21.0 3.7 %all-to-all-start = ((bf16[8,2,64,512]{3,2,1,0:T(8,128)(2,1)}), bf16[8,2,64,512]{3,2,1,0:T(8,128)(2,1)S(1)}, u32[]{:S(2)}, u32[]{:S(2)}) async-start(bf16[8,2,64,512]{3,2,1,0:T(8,128)(2,1)} %pair.1), calls=%async_computation | async-start | bytes 2097152 | tf_op jit(solution)/shard_map/all_to_all | solution.py:251
  24.7 0.0 all-gather.2.cloned.1.call-start
  24.8 0.2 reshape.29.idx
  25.0 0.0 copy-start.4
  25.0 1.2 copy-done.4
  26.2 1.0 norm.1
  27.2 0.7 copy-done.9
  27.9 0.8 copy-done.11
  28.7 3.3 %pick.1 = (bf16[192,1024]{1,0:T(8,128)(2,1)S(1)}, bf16[192,1024]{1,0:T(8,128)(2,1)S(1)}) custom-call(s32[5]{0:T(128)S(1)} %stack.23.meta, s32[8,48,1]{2,1,0:T(8,128)S(1)} %reshape.29.idx, bf16[1024,512]{1,0:T(8,128)(2,1)S(1)} %copy-done.2, bf16[1024,512]{1,0:T(8,128)(2,1)S(1)} %copy-done.3), custom_call_target="tpu_custom_call" | custom-call | flops 100663296 | bytes 3145728 | tf_op jit(solution)/shard_map/pick/pallas_call | solution.py:254
  32.0 0.0 copy-start.5
  32.0 0.7 copy-done.5
  32.7 0.8 copy-done.20
  33.5 9.2 %all-to-all-done.lines = bf16[8,2,64,512]{3,2,1,0:T(8,128)(2,1)S(1)} async-done(((bf16[8,2,64,512]{3,2,1,0:T(8,128)(2,1)}), bf16[8,2,64,512]{3,2,1,0:T(8,128)(2,1)S(1)}, u32[]{:S(2)}, u32[]{:S(2)}) %all-to-all-start) | async-done | bytes 1048608 | tf_op jit(solution)/shard_map/all_to_all | solution.py:251
  42.7 1.6 tighten.1
  44.4 0.0 all-gather.2.cloned.1.call-update
  44.4 0.0 reduce-scatter.2.cloned.1.call-start
  44.4 8.3 %collective-permute-start.4 = (bf16[192,1024]{1,0:T(8,128)(2,1)S(1)}, bf16[192,1024]{1,0:T(8,128)(2,1)S(1)}, u32[]{:S(2)}, u32[]{:S(2)}) collective-permute-start(bf16[192,1024]{1,0:T(8,128)(2,1)S(1)} %copy-done.21), channel_id=1, source_target_pairs={{0,1},{1,0},{2,3},{3,2},{4,5},{5,4},{6,7},{7,6},{8,9},{9,8},{10,11... | collective-permute-start | bytes 1179656 | tf_op jit(solution)/shard_map/ppermute | solution.py:260
  52.8 4.4 %collective-permute-start.1 = (bf16[48,3584]{1,0:T(8,128)(2,1)S(1)}, bf16[48,3584]{1,0:T(8,128)(2,1)S(1)}, u32[]{:S(2)}, u32[]{:S(2)}) collective-permute-start(bf16[48,3584]{1,0:T(8,128)(2,1)S(1)} %copy-done.10), channel_id=1, source_target_pairs={{0,6},{2,0},{4,2},{6,4},{1,7},{3,1},{5,3},{7,5},{8,14},{10,8},{12,... | collective-permute-start | bytes 1032200 | tf_op jit(solution)/shard_map/ppermute | solution.py:263
  57.2 2.4 %collective-permute-start.2 = (bf16[48,3584]{1,0:T(8,128)(2,1)S(1)}, bf16[48,3584]{1,0:T(8,128)(2,1)S(1)}, u32[]{:S(2)}, u32[]{:S(2)}) collective-permute-start(bf16[48,3584]{1,0:T(8,128)(2,1)S(1)} %copy-done.10), channel_id=1, source_target_pairs={{0,4},{2,6},{4,0},{6,2},{1,5},{3,7},{5,1},{7,3},{8,12},{10,14},{12... | collective-permute-start | bytes 1032200 | tf_op jit(solution)/shard_map/ppermute | solution.py:263
  59.6 6.9 %collective-permute-done.4.other = bf16[192,1024]{1,0:T(8,128)(2,1)S(1)} collective-permute-done((bf16[192,1024]{1,0:T(8,128)(2,1)S(1)}, bf16[192,1024]{1,0:T(8,128)(2,1)S(1)}, u32[]{:S(2)}, u32[]{:S(2)}) %collective-permute-start.4) | collective-permute-done | bytes 393248 | tf_op jit(solution)/shard_map/ppermute | solution.py:260
  66.5 0.7 copy-done.17
  67.1 0.6 join.1
  67.7 4.0 %collective-permute-start.5 = (bf16[192,1024]{1,0:T(8,128)(2,1)S(1)}, bf16[192,1024]{1,0:T(8,128)(2,1)S(1)}, u32[]{:S(2)}, u32[]{:S(2)}) collective-permute-start(bf16[192,1024]{1,0:T(8,128)(2,1)S(1)} %get-tuple-element.29.refs_4_), channel_id=1, source_target_pairs={{0,6},{2,0},{4,2},{6,4},{1,7},{3,1},{5,3},{7,5},{8,14},{10,8},{12,... | collective-permute-start | bytes 1179656 | tf_op jit(solution)/shard_map/ppermute | solution.py:263
  71.8 2.4 %collective-permute-start.6 = (bf16[192,1024]{1,0:T(8,128)(2,1)S(1)}, bf16[192,1024]{1,0:T(8,128)(2,1)S(1)}, u32[]{:S(2)}, u32[]{:S(2)}) collective-permute-start(bf16[192,1024]{1,0:T(8,128)(2,1)S(1)} %get-tuple-element.29.refs_4_), channel_id=1, source_target_pairs={{0,4},{2,6},{4,0},{6,2},{1,5},{3,7},{5,1},{7,3},{8,12},{10,14},{12... | collective-permute-start | bytes 1179656 | tf_op jit(solution)/shard_map/ppermute | solution.py:263
  74.2 2.5 %collective-permute-start.7 = (bf16[192,1024]{1,0:T(8,128)(2,1)S(1)}, bf16[192,1024]{1,0:T(8,128)(2,1)S(1)}, u32[]{:S(2)}, u32[]{:S(2)}) collective-permute-start(bf16[192,1024]{1,0:T(8,128)(2,1)S(1)} %get-tuple-element.29.refs_4_), channel_id=1, source_target_pairs={{0,2},{2,4},{4,6},{6,0},{1,3},{3,5},{5,7},{7,1},{8,10},{10,12},{12... | collective-permute-start | bytes 1179656 | tf_op jit(solution)/shard_map/ppermute | solution.py:263
  76.7 0.0 collective-permute-done.1.refs_1_
  76.7 4.8 %collective-permute-start.8 = (bf16[192,1024]{1,0:T(8,128)(2,1)S(1)}, bf16[192,1024]{1,0:T(8,128)(2,1)S(1)}, u32[]{:S(2)}, u32[]{:S(2)}) collective-permute-start(bf16[192,1024]{1,0:T(8,128)(2,1)S(1)} %get-tuple-element.32.res_own), channel_id=1, source_target_pairs={{8,0},{10,2},{12,4},{14,6},{24,16},{26,18},{28,20},{30,22},{40,32}... | collective-permute-start | bytes 1179656 | tf_op jit(solution)/shard_map/ppermute | solution.py:269
  81.6 0.0 collective-permute-done.2.refs_2_
  81.6 3.4 %collective-permute-start.3 = (bf16[48,3584]{1,0:T(8,128)(2,1)S(1)}, bf16[48,3584]{1,0:T(8,128)(2,1)S(1)}, u32[]{:S(2)}, u32[]{:S(2)}) collective-permute-start(bf16[48,3584]{1,0:T(8,128)(2,1)S(1)} %copy-done.10), channel_id=1, source_target_pairs={{0,2},{2,4},{4,6},{6,0},{1,3},{3,5},{5,7},{7,1},{8,10},{10,12},{12... | collective-permute-start | bytes 1032200 | tf_op jit(solution)/shard_map/ppermute | solution.py:263
  85.0 17.0 %collective-permute-done.3.refs_3_ = bf16[48,3584]{1,0:T(8,128)(2,1)S(1)} collective-permute-done((bf16[48,3584]{1,0:T(8,128)(2,1)S(1)}, bf16[48,3584]{1,0:T(8,128)(2,1)S(1)}, u32[]{:S(2)}, u32[]{:S(2)}) %collective-permute-start.3) | collective-permute-done | bytes 344096 | tf_op jit(solution)/shard_map/ppermute | solution.py:263
  102.0 0.0 collective-permute-done.7.refs_7_
  102.0 1.0 choose.1
  103.0 0.0 collective-permute-done.8.res_oth
  103.0 0.0 copy-start.7
  103.0 0.8 copy-done.7
  103.8 2.4 %collective-permute-start.9 = (bf16[192,4096]{1,0:T(8,128)(2,1)S(1)}, bf16[192,4096]{1,0:T(8,128)(2,1)S(1)}, u32[]{:S(2)}, u32[]{:S(2)}) collective-permute-start(bf16[192,4096]{1,0:T(8,128)(2,1)S(1)} %get-tuple-element.33), channel_id=1, source_target_pairs={{0,8},{8,0},{1,9},{9,1},{2,10},{10,2},{3,11},{11,3},{4,12},{12,4},... | collective-permute-start | bytes 4718600 | tf_op jit(solution)/shard_map/ppermute | solution.py:275
  106.2 3.0 %collective-permute-done.9.oth = bf16[192,4096]{1,0:T(8,128)(2,1)S(1)} collective-permute-done((bf16[192,4096]{1,0:T(8,128)(2,1)S(1)}, bf16[192,4096]{1,0:T(8,128)(2,1)S(1)}, u32[]{:S(2)}, u32[]{:S(2)}) %collective-permute-start.9) | collective-permute-done | bytes 1572896 | tf_op jit(solution)/shard_map/ppermute | solution.py:275
  109.2 0.2 all-gather.2.cloned.1.call-done
  109.4 0.7 copy-done.18
  110.1 6.6 %forward.1 = (f32[384,1024]{1,0:T(8,128)S(1)}, bf16[384,1024]{1,0:T(8,128)(2,1)S(1)}) custom-call(s32[5]{0:T(128)S(1)} %copy-done.18, bf16[192,4096]{1,0:T(8,128)(2,1)S(1)} %get-tuple-element.30.own, bf16[192,4096]{1,0:T(8,128)(2,1)S(1)} %collective-permute-done.9.oth, bf16[8,1024,512]{2,1,0:T(8,128)(2,1)} %bitcast.10), custom_call_target="tpu_custom_call" | custom-call | flops 3221225472 | bytes 13631488 | tf_op jit(solution)/shard_map/forward/pallas_call | solution.py:278
  116.7 2.4 %collective-permute-start.10 = (bf16[384,1024]{1,0:T(8,128)(2,1)S(1)}, bf16[384,1024]{1,0:T(8,128)(2,1)S(1)}, u32[]{:S(2)}, u32[]{:S(2)}) collective-permute-start(bf16[384,1024]{1,0:T(8,128)(2,1)S(1)} %get-tuple-element.36), channel_id=1, source_target_pairs={{8,0},{10,2},{12,4},{14,6},{24,16},{26,18},{28,20},{30,22},{40,32}... | collective-permute-start | bytes 2359304 | tf_op jit(solution)/shard_map/ppermute | solution.py:287
  119.0 1.7 collective-permute-done.10.teach
  120.7 8.4 %backward.1 = (bf16[192,3584]{1,0:T(8,128)(2,1)S(1)}, bf16[192,3584]{1,0:T(8,128)(2,1)S(1)}, f32[1,3584]{1,0:T(1,128)S(1)}) custom-call(s32[5]{0:T(128)S(1)} %copy-done.18, f32[384,1024]{1,0:T(8,128)S(1)} %get-tuple-element.35.pred, bf16[384,1024]{1,0:T(8,128)(2,1)S(1)} %collective-permute-done.10.teach, bf16[192,1024]{1,0:T(8,128)(2,1)S(1)} %get-tuple-element.32.res_own, ...), custom_call_target="tpu_custom_call" | custom-call | flops 2818572288 | bytes 16777216 | tf_op jit(solution)/shard_map/backward/pallas_call | solution.py:288
  129.1 1.3 collective-permute-start.12
  130.4 1.3 collective-permute-start.11
  131.7 2.8 %collective-permute-done.11 = f32[28,128]{1,0:T(8,128)S(1)} collective-permute-done((f32[28,128]{1,0:T(8,128)S(1)}, f32[28,128]{1,0:T(8,128)S(1)}, u32[]{:S(2)}, u32[]{:S(2)}) %collective-permute-start.11) | collective-permute-done | bytes 14368 | tf_op jit(solution)/shard_map/ppermute | solution.py:299
  134.6 2.6 %broadcast_select_fusion = bf16[192,3584]{1,0:T(8,128)(2,1)} fusion(bf16[192,3584]{1,0:T(8,128)(2,1)S(1)} %get-tuple-element.41, bf16[192,3584]{1,0:T(8,128)(2,1)} %collective-permute-done.12, pred[]{:T(512)S(6)} %eq.3), kind=kLoop, calls=%fused_computation | loop fusion | flops 688128 | bytes 4128769 | tf_op jit(solution)/shard_map/jit(_where)/select_n | solution.py:304
  137.2 0.0 reduce-scatter.2.cloned.1.call-update
  137.3 14.9 %all_to_all.15 = f32[16,28,128]{2,1,0:T(8,128)S(1)} all-to-all(f32[16,28,128]{2,1,0:T(8,128)S(1)} %broadcast_in_dim.4), channel_id=1, replica_groups={{0,64,128,192,2,66,130,194,4,68,132,196,6,70,134,198},{8,72,136,200,10,..., dimensions={0} | all-to-all | bytes 458752 | tf_op jit(solution)/shard_map/all_to_all | solution.py:302
  152.2 0.7 broadcast_in_dim.5
  152.9 13.9 %all-to-all-start.2 = ((f32[16,28,128]{2,1,0:T(8,128)}), f32[16,28,128]{2,1,0:T(8,128)S(1)}, u32[]{:S(2)}, u32[]{:S(2)}) async-start(f32[16,28,128]{2,1,0:T(8,128)} %broadcast_in_dim.5), calls=%async_computation.2 | async-start | bytes 524288 | tf_op jit(solution)/shard_map/all_to_all | solution.py:221
  166.8 0.6 reduce-scatter.2.cloned.1.call-done.summed
  167.4 1.0 copy-done.13
  168.4 2.4 %finish.1 = bf16[128,3584]{1,0:T(8,128)(2,1)} custom-call(s32[5]{0:T(128)S(1)} %copy-done.19, s32[1,384]{1,0:T(1,128)S(1)} %reshape.28.idx, bf16[48,3584]{1,0:T(8,128)(2,1)S(1)} %copy-done.13, bf16[48,3584]{1,0:T(8,128)(2,1)S(1)} %copy-done.12, f32[1,3584]{1,0:T(1,128)S(1)} %reshape.25.gain.gain_ref), custom_call_target="tpu_custom_call" | custom-call | flops 44040192 | bytes 4194304 | tf_op jit(solution)/shard_map/finish/pallas_call | solution.py:305
  170.9 7.9 %all-to-all-done.2 = f32[16,28,128]{2,1,0:T(8,128)S(1)} async-done(((f32[16,28,128]{2,1,0:T(8,128)}), f32[16,28,128]{2,1,0:T(8,128)S(1)}, u32[]{:S(2)}, u32[]{:S(2)}) %all-to-all-start.2) | async-done | bytes 229408 | tf_op jit(solution)/shard_map/all_to_all | solution.py:221
  178.8 0.6 multiply_reduce_fusion
  180.0 0.6 multiply_bitcast_fusion
  (46 shorter events, 0.2 us)
Async XLA Ops:
  8.0 9.7 %collective-permute-start = (bf16[64,512]{1,0:T(8,128)(2,1)S(1)}, bf16[64,512]{1,0:T(8,128)(2,1)S(1)}, u32[]{:S(2)}, u32[]{:S(2)}) collective-permute-start(bf16[64,512]{1,0:T(8,128)(2,1)S(1)} %pad_select_fusion), channel_id=1, source_target_pairs={{0,8},{8,0},{1,9},{9,1},{2,10},{10,2},{3,11},{11,3},{4,12},{12,4},... | collective-permute-start | bytes 196616 | tf_op jit(solution)/shard_map/ppermute | solution.py:247
  16.9 25.8 %copy-start.16 = (s32[5]{0:T(128)}, s32[5]{0:T(128)S(1)}, u32[]{:S(2)}) copy-start(s32[5]{0:T(128)S(1)} %stack.23.meta) | copy-start | bytes 64
  17.7 0.8 copy-start.14
  18.6 0.8 copy-start.15
  19.4 5.4 %copy-start.22 = (f32[3584]{0:T(1024)S(1)}, f32[3584]{0:T(1024)}, u32[]{:S(2)}) copy-start(f32[3584]{0:T(1024)} %param.12) | copy-start | bytes 43012
  19.4 5.4 %copy-start.23 = (s32[384]{0:T(512)S(1)}, s32[384]{0:T(512)}, u32[]{:S(2)}) copy-start(s32[384]{0:T(512)} %param.13) | copy-start | bytes 4612
  21.0 7.7 %copy-start.2 = (bf16[1024,512]{1,0:T(8,128)(2,1)S(1)}, bf16[1024,512]{1,0:T(8,128)(2,1)}, u32[]{:S(2)}) copy-start(bf16[1024,512]{1,0:T(8,128)(2,1)} %context.1) | copy-start | bytes 3145732
  21.0 7.7 %copy-start.3 = (bf16[1024,512]{1,0:T(8,128)(2,1)S(1)}, bf16[1024,512]{1,0:T(8,128)(2,1)}, u32[]{:S(2)}) copy-start(bf16[1024,512]{1,0:T(8,128)(2,1)} %residual.1) | copy-start | bytes 3145732
  21.0 21.7 %all-to-all-start = ((bf16[8,2,64,512]{3,2,1,0:T(8,128)(2,1)}), bf16[8,2,64,512]{3,2,1,0:T(8,128)(2,1)S(1)}, u32[]{:S(2)}, u32[]{:S(2)}) async-start(bf16[8,2,64,512]{3,2,1,0:T(8,128)(2,1)} %pair.1), calls=%async_computation | async-start | bytes 2097152 | tf_op jit(solution)/shard_map/all_to_all | solution.py:251
  24.7 84.7 %all-gather.2.cloned.1.call-start = ((), (), s32[]{:S(2)}) async-start(), calls=%async_computation.4 | async-start | bytes 9437184 | tf_op jit(solution)/shard_map/all_gather | solution.py:258
  25.0 1.2 copy-start.4
  27.2 0.7 copy-start.9
  27.9 0.8 copy-start.11
  32.0 0.7 copy-start.5
  32.7 0.8 copy-start.20
  33.5 19.3 %copy-start.10 = (bf16[48,3584]{1,0:T(8,128)(2,1)S(1)}, bf16[48,3584]{1,0:T(8,128)(2,1)}, u32[]{:S(2)}) copy-start(bf16[48,3584]{1,0:T(8,128)(2,1)} %copy-done.9) | copy-start | bytes 1032196
  42.7 1.7 copy-start.21
  42.7 23.7 %copy-start.6 = (bf16[192,1024]{1,0:T(8,128)(2,1)S(1)}, bf16[192,1024]{1,0:T(8,128)(2,1)}, u32[]{:S(2)}) copy-start(bf16[192,1024]{1,0:T(8,128)(2,1)} %copy-done.5) | copy-start | bytes 1179652
  44.4 123.1 %reduce-scatter.2.cloned.1.call-start = ((), (), s32[]{:S(2)}) async-start(), calls=%async_computation.5 | async-start | bytes 1720320 | tf_op jit(solution)/shard_map/reduce_scatter | solution.py:304
  44.4 22.0 %collective-permute-start.4 = (bf16[192,1024]{1,0:T(8,128)(2,1)S(1)}, bf16[192,1024]{1,0:T(8,128)(2,1)S(1)}, u32[]{:S(2)}, u32[]{:S(2)}) collective-permute-start(bf16[192,1024]{1,0:T(8,128)(2,1)S(1)} %copy-done.21), channel_id=1, source_target_pairs={{0,1},{1,0},{2,3},{3,2},{4,5},{5,4},{6,7},{7,6},{8,9},{9,8},{10,11... | collective-permute-start | bytes 1179656 | tf_op jit(solution)/shard_map/ppermute | solution.py:260
  52.8 24.0 %collective-permute-start.1 = (bf16[48,3584]{1,0:T(8,128)(2,1)S(1)}, bf16[48,3584]{1,0:T(8,128)(2,1)S(1)}, u32[]{:S(2)}, u32[]{:S(2)}) collective-permute-start(bf16[48,3584]{1,0:T(8,128)(2,1)S(1)} %copy-done.10), channel_id=1, source_target_pairs={{0,6},{2,0},{4,2},{6,4},{1,7},{3,1},{5,3},{7,5},{8,14},{10,8},{12,... | collective-permute-start | bytes 1032200 | tf_op jit(solution)/shard_map/ppermute | solution.py:263
  57.2 24.4 %collective-permute-start.2 = (bf16[48,3584]{1,0:T(8,128)(2,1)S(1)}, bf16[48,3584]{1,0:T(8,128)(2,1)S(1)}, u32[]{:S(2)}, u32[]{:S(2)}) collective-permute-start(bf16[48,3584]{1,0:T(8,128)(2,1)S(1)} %copy-done.10), channel_id=1, source_target_pairs={{0,4},{2,6},{4,0},{6,2},{1,5},{3,7},{5,1},{7,3},{8,12},{10,14},{12... | collective-permute-start | bytes 1032200 | tf_op jit(solution)/shard_map/ppermute | solution.py:263
  66.5 0.7 copy-start.17
  67.7 34.3 %collective-permute-start.5 = (bf16[192,1024]{1,0:T(8,128)(2,1)S(1)}, bf16[192,1024]{1,0:T(8,128)(2,1)S(1)}, u32[]{:S(2)}, u32[]{:S(2)}) collective-permute-start(bf16[192,1024]{1,0:T(8,128)(2,1)S(1)} %get-tuple-element.29.refs_4_), channel_id=1, source_target_pairs={{0,6},{2,0},{4,2},{6,4},{1,7},{3,1},{5,3},{7,5},{8,14},{10,8},{12,... | collective-permute-start | bytes 1179656 | tf_op jit(solution)/shard_map/ppermute | solution.py:263
  71.8 30.2 %collective-permute-start.6 = (bf16[192,1024]{1,0:T(8,128)(2,1)S(1)}, bf16[192,1024]{1,0:T(8,128)(2,1)S(1)}, u32[]{:S(2)}, u32[]{:S(2)}) collective-permute-start(bf16[192,1024]{1,0:T(8,128)(2,1)S(1)} %get-tuple-element.29.refs_4_), channel_id=1, source_target_pairs={{0,4},{2,6},{4,0},{6,2},{1,5},{3,7},{5,1},{7,3},{8,12},{10,14},{12... | collective-permute-start | bytes 1179656 | tf_op jit(solution)/shard_map/ppermute | solution.py:263
  74.2 27.8 %collective-permute-start.7 = (bf16[192,1024]{1,0:T(8,128)(2,1)S(1)}, bf16[192,1024]{1,0:T(8,128)(2,1)S(1)}, u32[]{:S(2)}, u32[]{:S(2)}) collective-permute-start(bf16[192,1024]{1,0:T(8,128)(2,1)S(1)} %get-tuple-element.29.refs_4_), channel_id=1, source_target_pairs={{0,2},{2,4},{4,6},{6,0},{1,3},{3,5},{5,7},{7,1},{8,10},{10,12},{12... | collective-permute-start | bytes 1179656 | tf_op jit(solution)/shard_map/ppermute | solution.py:263
  76.7 26.3 %collective-permute-start.8 = (bf16[192,1024]{1,0:T(8,128)(2,1)S(1)}, bf16[192,1024]{1,0:T(8,128)(2,1)S(1)}, u32[]{:S(2)}, u32[]{:S(2)}) collective-permute-start(bf16[192,1024]{1,0:T(8,128)(2,1)S(1)} %get-tuple-element.32.res_own), channel_id=1, source_target_pairs={{8,0},{10,2},{12,4},{14,6},{24,16},{26,18},{28,20},{30,22},{40,32}... | collective-permute-start | bytes 1179656 | tf_op jit(solution)/shard_map/ppermute | solution.py:269
  81.6 20.4 %collective-permute-start.3 = (bf16[48,3584]{1,0:T(8,128)(2,1)S(1)}, bf16[48,3584]{1,0:T(8,128)(2,1)S(1)}, u32[]{:S(2)}, u32[]{:S(2)}) collective-permute-start(bf16[48,3584]{1,0:T(8,128)(2,1)S(1)} %copy-done.10), channel_id=1, source_target_pairs={{0,2},{2,4},{4,6},{6,0},{1,3},{3,5},{5,7},{7,1},{8,10},{10,12},{12... | collective-permute-start | bytes 1032200 | tf_op jit(solution)/shard_map/ppermute | solution.py:263
  103.0 13.7 %copy-start = (bf16[192,4096]{1,0:T(8,128)(2,1)}, bf16[192,4096]{1,0:T(8,128)(2,1)S(1)}, u32[]{:S(2)}) copy-start(bf16[192,4096]{1,0:T(8,128)(2,1)S(1)} %get-tuple-element.30.own) | copy-start | bytes 4718596
  103.0 0.8 copy-start.7
  103.8 5.4 %collective-permute-start.9 = (bf16[192,4096]{1,0:T(8,128)(2,1)S(1)}, bf16[192,4096]{1,0:T(8,128)(2,1)S(1)}, u32[]{:S(2)}, u32[]{:S(2)}) collective-permute-start(bf16[192,4096]{1,0:T(8,128)(2,1)S(1)} %get-tuple-element.33), channel_id=1, source_target_pairs={{0,8},{8,0},{1,9},{9,1},{2,10},{10,2},{3,11},{11,3},{4,12},{12,4},... | collective-permute-start | bytes 4718600 | tf_op jit(solution)/shard_map/ppermute | solution.py:275
  109.2 7.4 %copy-start.1 = (bf16[192,4096]{1,0:T(8,128)(2,1)}, bf16[192,4096]{1,0:T(8,128)(2,1)S(1)}, u32[]{:S(2)}) copy-start(bf16[192,4096]{1,0:T(8,128)(2,1)S(1)} %collective-permute-done.9.oth) | copy-start | bytes 4718596
  109.4 0.7 copy-start.18
  110.1 10.6 %copy-start.8 = (bf16[192,1024]{1,0:T(8,128)(2,1)S(1)}, bf16[192,1024]{1,0:T(8,128)(2,1)}, u32[]{:S(2)}) copy-start(bf16[192,1024]{1,0:T(8,128)(2,1)} %copy-done.7) | copy-start | bytes 1179652
  116.7 4.0 %collective-permute-start.10 = (bf16[384,1024]{1,0:T(8,128)(2,1)S(1)}, bf16[384,1024]{1,0:T(8,128)(2,1)S(1)}, u32[]{:S(2)}, u32[]{:S(2)}) collective-permute-start(bf16[384,1024]{1,0:T(8,128)(2,1)S(1)} %get-tuple-element.36), channel_id=1, source_target_pairs={{8,0},{10,2},{12,4},{14,6},{24,16},{26,18},{28,20},{30,22},{40,32}... | collective-permute-start | bytes 2359304 | tf_op jit(solution)/shard_map/ppermute | solution.py:287
  129.1 5.5 %collective-permute-start.12 = (bf16[192,3584]{1,0:T(8,128)(2,1)S(1)}, bf16[192,3584]{1,0:T(8,128)(2,1)}, u32[]{:S(2)}, u32[]{:S(2)}) collective-permute-start(bf16[192,3584]{1,0:T(8,128)(2,1)S(1)} %get-tuple-element.39), channel_id=1, source_target_pairs={{0,8},{2,10},{4,12},{6,14},{16,24},{18,26},{20,28},{22,30},{32,40}... | collective-permute-start | bytes 4128776 | tf_op jit(solution)/shard_map/ppermute | solution.py:301
  130.4 4.1 %collective-permute-start.11 = (f32[28,128]{1,0:T(8,128)S(1)}, f32[28,128]{1,0:T(8,128)S(1)}, u32[]{:S(2)}, u32[]{:S(2)}) collective-permute-start(f32[28,128]{1,0:T(8,128)S(1)} %bitcast.12), channel_id=1, source_target_pairs={{0,8},{2,10},{4,12},{6,14},{16,24},{18,26},{20,28},{22,30},{32,40}... | collective-permute-start | bytes 43016 | tf_op jit(solution)/shard_map/ppermute | solution.py:299
  137.2 29.6 %copy-start.24 = (s32[384]{0:T(512)S(1)}, s32[384]{0:T(512)}, u32[]{:S(2)}) copy-start(s32[384]{0:T(512)} %param.13) | copy-start | bytes 4612
  137.2 30.2 %copy-start.12 = (bf16[48,3584]{1,0:T(8,128)(2,1)S(1)}, bf16[48,3584]{1,0:T(8,128)(2,1)}, u32[]{:S(2)}) copy-start(bf16[48,3584]{1,0:T(8,128)(2,1)} %copy-done.11) | copy-start | bytes 1032196
  137.2 30.2 %copy-start.19 = (s32[5]{0:T(128)S(1)}, s32[5]{0:T(128)}, u32[]{:S(2)}) copy-start(s32[5]{0:T(128)} %copy-done.16) | copy-start | bytes 64
  152.9 25.8 %all-to-all-start.2 = ((f32[16,28,128]{2,1,0:T(8,128)}), f32[16,28,128]{2,1,0:T(8,128)S(1)}, u32[]{:S(2)}, u32[]{:S(2)}) async-start(f32[16,28,128]{2,1,0:T(8,128)} %broadcast_in_dim.5), calls=%async_computation.2 | async-start | bytes 524288 | tf_op jit(solution)/shard_map/all_to_all | solution.py:221
  167.4 1.0 copy-start.13
Sparse Core Ops, SparseCore 0:
  44.5 64.8 all-gather.1
  137.4 30.0 reduce-scatter.1

commit v4 on v3

--- a/solution.py
+++ b/solution.py
@@ -26,18 +26,8 @@
 Y_ON_0 = [[dev(y, z, 0, x) for y in range(NY)] for z in range(NZ) for x in range(NX)] + [
     [dev(y, z, 1, x) for z in range(NZ)] for y in range(NY) for x in range(NX)
 ]
-FIRST = [
-    [dev(h * 4 + y, z, c, x) for x in range(NX) for y in range(4)]
-    for h in range(2)
-    for z in range(NZ)
-    for c in range(NC)
-]
-SECOND = [
-    [dev(h * 4 + y, z, c, x) for h in range(2) for z in range(NZ)]
-    for c in range(NC)
-    for x in range(NX)
-    for y in range(4)
-]
+FIRST = [[dev(y, z, c, x) for x in range(NX) for y in range(NY)] for z in range(NZ) for c in range(NC)]
+SECOND = [[dev(y, z, c, x) for z in range(NZ)] for c in range(NC) for x in range(NX) for y in range(NY)]
 SWAP = [(0, 1), (1, 0)]
 DOWN = [(dev(y, z, 0, x), dev(y, z, 1, x)) for y, z, x in CHIPS]
 UP = [(b, a) for a, b in DOWN]
@@ -297,7 +287,7 @@
 
     gain_part = gain_part.reshape(28, 128)
     gain_part = jnp.where(first, gain_part, lax.ppermute(gain_part, AXES, DOWN))
-    gain_wide = jnp.broadcast_to(gain_part[None], (16, 28, 128))
+    gain_wide = jnp.broadcast_to(gain_part[None], (32, 28, 128))
     gain_wide, handed = lax.optimization_barrier((gain_wide, lax.ppermute(term_oth, AXES, DOWN)))
     gain_part = jnp.sum(lax.all_to_all(gain_wide, AXES, 0, 0, axis_index_groups=FIRST), axis=0)
 
@@ -306,7 +296,7 @@
         finish, [((own_rows, width), BF16)], [SMEM] + [VMEM] * 4, [], 2 * 128 * 48 * width, 4 << 20, "finish"
     )(meta, idx_row, summed, hid, gain_row)
 
-    gathered, grad_hidden = lax.optimization_barrier((spread(gain_part, AXES, 16, SECOND), grad_hidden))
+    gathered, grad_hidden = lax.optimization_barrier((spread(gain_part, AXES, 8, SECOND), grad_hidden))
     grad_gain = jnp.sum(gathered, axis=0).reshape(width)
     gain_update = grad_gain * lax.rsqrt(jnp.mean(grad_gain * grad_gain) + EPS)
     return (grad_hidden, gain_update)

time: 190 us -> 190 us (level)
  blocking collectives: 14.9 us -> 22.5 us
  starting transfers between devices: 66.2 us -> 62.8 us
  waiting for transfers between devices: 50 us -> 46.7 us
    all_to_all x1, blocking collectives: 14.9 us -> 22.5 us  [body(): lax.all_to_all(gain_wide, AXES, 0, 0, axis_index_groups=FIRST)]
    all_to_all x1, starting transfers between devices: 13.9 us -> 10.5 us  [spread(): lax.all_to_all(jnp.broadcast_to(block[None], (size,) + block.shape), axis...]
    all_to_all x1, waiting for transfers between devices: 7.85 us -> 5.09 us  [spread(): lax.all_to_all(jnp.broadcast_to(block[None], (size,) + block.shape), axis...]
  transfers between devices with their start and end apart: 17 -> 17, of which waited for: 10 -> 9; matrix products, arithmetic and copies ran while one was open for 1% -> 1% of each run, Pallas kernels for 4% -> 4%
where the time goes in v4:
time: 190 us; the launch traced here: 188 us
  starting transfers between devices  62.8 us (33%)
  waiting for transfers between devices  46.7 us (25%)
  Pallas kernels  26.4 us (14%)
  blocking collectives  22.5 us (12%)
  between operations  15.1 us (8%)
  local copies, waits for them, and re-layouts  10 us (5%)
  other arithmetic  4.77 us (3%)
    all_to_all x1, blocking collectives, body(): lax.all_to_all(gain_wide, AXES, 0, 0, axis_index_groups=FIRST)  22.5 us
    ppermute x6, starting transfers between devices, around(): lax.ppermute(block, 'x', [(i, (i - d) % NX) for i in range(NX)])  19.2 us
    ppermute x6, waiting for transfers between devices, around(): lax.ppermute(block, 'x', [(i, (i - d) % NX) for i in range(NX)])  17 us
    all_to_all x1, starting transfers between devices, spread(): lax.all_to_all(jnp.broadcast_to(block[None], (size,) + block.shape), axis...  10.5 us
    all_to_all x1, waiting for transfers between devices, body(): lines = lax.all_to_all(pair, AXES, 0, 0, axis_index_groups=Z_ON_0)  9.2 us
    unnamed x50, local copies, waits for them, and re-layouts  9.02 us
    ppermute x1, starting transfers between devices, body(): lax.ppermute(jnp.where(first, w_out, jnp.pad(w_proj, ((0, 8), (0, 0)))),...  8.82 us
    pallas_call x1, Pallas kernels, body(): call(backward, [((192, width), BF16), ((192, width), BF16), ((1, width),...  8.37 us
  transfers between devices with their start and end apart: 17, of which 9 were waited for; matrix products, arithmetic and copies ran while one was open for 1% of the time, Pallas kernels for 4%

profile of v4, /device:TPU:1, one launch (start us, length us, event | category | flops | bytes accessed | tf_op | source)
XLA Modules:
  0.0 188.3 jit_solution(16511376095527456197)
XLA Ops:
  7.2 0.8 pad_select_fusion
  8.0 8.8 %collective-permute-start = (bf16[64,512]{1,0:T(8,128)(2,1)S(1)}, bf16[64,512]{1,0:T(8,128)(2,1)S(1)}, u32[]{:S(2)}, u32[]{:S(2)}) collective-permute-start(bf16[64,512]{1,0:T(8,128)(2,1)S(1)} %pad_select_fusion), channel_id=1, source_target_pairs={{0,8},{8,0},{1,9},{9,1},{2,10},{10,2},{3,11},{11,3},{4,12},{12,4},... | collective-permute-start | bytes 196616 | tf_op jit(solution)/shard_map/ppermute | solution.py:237
  16.9 0.1 stack.23.meta
  16.9 0.8 collective-permute-done.got
  17.7 0.8 copy-done.14
  18.6 0.8 copy-done.15
  19.4 1.6 pair.1
  21.0 3.7 %all-to-all-start = ((bf16[8,2,64,512]{3,2,1,0:T(8,128)(2,1)}), bf16[8,2,64,512]{3,2,1,0:T(8,128)(2,1)S(1)}, u32[]{:S(2)}, u32[]{:S(2)}) async-start(bf16[8,2,64,512]{3,2,1,0:T(8,128)(2,1)} %pair.1), calls=%async_computation | async-start | bytes 2097152 | tf_op jit(solution)/shard_map/all_to_all | solution.py:241
  24.7 0.0 all-gather.2.cloned.1.call-start
  24.8 0.2 reshape.29.idx
  25.0 0.0 copy-start.4
  25.0 1.2 copy-done.4
  26.2 1.0 norm.1
  27.2 0.7 copy-done.9
  27.9 0.8 copy-done.11
  28.7 3.3 %pick.1 = (bf16[192,1024]{1,0:T(8,128)(2,1)S(1)}, bf16[192,1024]{1,0:T(8,128)(2,1)S(1)}) custom-call(s32[5]{0:T(128)S(1)} %stack.23.meta, s32[8,48,1]{2,1,0:T(8,128)S(1)} %reshape.29.idx, bf16[1024,512]{1,0:T(8,128)(2,1)S(1)} %copy-done.2, bf16[1024,512]{1,0:T(8,128)(2,1)S(1)} %copy-done.3), custom_call_target="tpu_custom_call" | custom-call | flops 100663296 | bytes 3145728 | tf_op jit(solution)/shard_map/pick/pallas_call | solution.py:244
  32.0 0.0 copy-start.5
  32.0 0.7 copy-done.5
  32.7 0.8 copy-done.20
  33.5 9.2 %all-to-all-done.lines = bf16[8,2,64,512]{3,2,1,0:T(8,128)(2,1)S(1)} async-done(((bf16[8,2,64,512]{3,2,1,0:T(8,128)(2,1)}), bf16[8,2,64,512]{3,2,1,0:T(8,128)(2,1)S(1)}, u32[]{:S(2)}, u32[]{:S(2)}) %all-to-all-start) | async-done | bytes 1048608 | tf_op jit(solution)/shard_map/all_to_all | solution.py:241
  42.7 1.6 tighten.1
  44.4 0.0 all-gather.2.cloned.1.call-update
  44.4 0.0 reduce-scatter.2.cloned.1.call-start
  44.4 8.3 %collective-permute-start.4 = (bf16[192,1024]{1,0:T(8,128)(2,1)S(1)}, bf16[192,1024]{1,0:T(8,128)(2,1)S(1)}, u32[]{:S(2)}, u32[]{:S(2)}) collective-permute-start(bf16[192,1024]{1,0:T(8,128)(2,1)S(1)} %copy-done.21), channel_id=1, source_target_pairs={{0,1},{1,0},{2,3},{3,2},{4,5},{5,4},{6,7},{7,6},{8,9},{9,8},{10,11... | collective-permute-start | bytes 1179656 | tf_op jit(solution)/shard_map/ppermute | solution.py:250
  52.8 4.4 %collective-permute-start.1 = (bf16[48,3584]{1,0:T(8,128)(2,1)S(1)}, bf16[48,3584]{1,0:T(8,128)(2,1)S(1)}, u32[]{:S(2)}, u32[]{:S(2)}) collective-permute-start(bf16[48,3584]{1,0:T(8,128)(2,1)S(1)} %copy-done.10), channel_id=1, source_target_pairs={{0,6},{2,0},{4,2},{6,4},{1,7},{3,1},{5,3},{7,5},{8,14},{10,8},{12,... | collective-permute-start | bytes 1032200 | tf_op jit(solution)/shard_map/ppermute | solution.py:253
  57.2 2.4 %collective-permute-start.2 = (bf16[48,3584]{1,0:T(8,128)(2,1)S(1)}, bf16[48,3584]{1,0:T(8,128)(2,1)S(1)}, u32[]{:S(2)}, u32[]{:S(2)}) collective-permute-start(bf16[48,3584]{1,0:T(8,128)(2,1)S(1)} %copy-done.10), channel_id=1, source_target_pairs={{0,4},{2,6},{4,0},{6,2},{1,5},{3,7},{5,1},{7,3},{8,12},{10,14},{12... | collective-permute-start | bytes 1032200 | tf_op jit(solution)/shard_map/ppermute | solution.py:253
  59.6 6.9 %collective-permute-done.4.other = bf16[192,1024]{1,0:T(8,128)(2,1)S(1)} collective-permute-done((bf16[192,1024]{1,0:T(8,128)(2,1)S(1)}, bf16[192,1024]{1,0:T(8,128)(2,1)S(1)}, u32[]{:S(2)}, u32[]{:S(2)}) %collective-permute-start.4) | collective-permute-done | bytes 393248 | tf_op jit(solution)/shard_map/ppermute | solution.py:250
  66.5 0.7 copy-done.17
  67.1 0.6 join.1
  67.7 4.0 %collective-permute-start.5 = (bf16[192,1024]{1,0:T(8,128)(2,1)S(1)}, bf16[192,1024]{1,0:T(8,128)(2,1)S(1)}, u32[]{:S(2)}, u32[]{:S(2)}) collective-permute-start(bf16[192,1024]{1,0:T(8,128)(2,1)S(1)} %get-tuple-element.29.refs_4_), channel_id=1, source_target_pairs={{0,6},{2,0},{4,2},{6,4},{1,7},{3,1},{5,3},{7,5},{8,14},{10,8},{12,... | collective-permute-start | bytes 1179656 | tf_op jit(solution)/shard_map/ppermute | solution.py:253
  71.8 2.4 %collective-permute-start.6 = (bf16[192,1024]{1,0:T(8,128)(2,1)S(1)}, bf16[192,1024]{1,0:T(8,128)(2,1)S(1)}, u32[]{:S(2)}, u32[]{:S(2)}) collective-permute-start(bf16[192,1024]{1,0:T(8,128)(2,1)S(1)} %get-tuple-element.29.refs_4_), channel_id=1, source_target_pairs={{0,4},{2,6},{4,0},{6,2},{1,5},{3,7},{5,1},{7,3},{8,12},{10,14},{12... | collective-permute-start | bytes 1179656 | tf_op jit(solution)/shard_map/ppermute | solution.py:253
  74.2 2.5 %collective-permute-start.7 = (bf16[192,1024]{1,0:T(8,128)(2,1)S(1)}, bf16[192,1024]{1,0:T(8,128)(2,1)S(1)}, u32[]{:S(2)}, u32[]{:S(2)}) collective-permute-start(bf16[192,1024]{1,0:T(8,128)(2,1)S(1)} %get-tuple-element.29.refs_4_), channel_id=1, source_target_pairs={{0,2},{2,4},{4,6},{6,0},{1,3},{3,5},{5,7},{7,1},{8,10},{10,12},{12... | collective-permute-start | bytes 1179656 | tf_op jit(solution)/shard_map/ppermute | solution.py:253
  76.7 0.0 collective-permute-done.1.refs_1_
  76.7 4.8 %collective-permute-start.8 = (bf16[192,1024]{1,0:T(8,128)(2,1)S(1)}, bf16[192,1024]{1,0:T(8,128)(2,1)S(1)}, u32[]{:S(2)}, u32[]{:S(2)}) collective-permute-start(bf16[192,1024]{1,0:T(8,128)(2,1)S(1)} %get-tuple-element.32.res_own), channel_id=1, source_target_pairs={{8,0},{10,2},{12,4},{14,6},{24,16},{26,18},{28,20},{30,22},{40,32}... | collective-permute-start | bytes 1179656 | tf_op jit(solution)/shard_map/ppermute | solution.py:259
  81.6 0.0 collective-permute-done.2.refs_2_
  81.6 3.4 %collective-permute-start.3 = (bf16[48,3584]{1,0:T(8,128)(2,1)S(1)}, bf16[48,3584]{1,0:T(8,128)(2,1)S(1)}, u32[]{:S(2)}, u32[]{:S(2)}) collective-permute-start(bf16[48,3584]{1,0:T(8,128)(2,1)S(1)} %copy-done.10), channel_id=1, source_target_pairs={{0,2},{2,4},{4,6},{6,0},{1,3},{3,5},{5,7},{7,1},{8,10},{10,12},{12... | collective-permute-start | bytes 1032200 | tf_op jit(solution)/shard_map/ppermute | solution.py:253
  85.0 17.0 %collective-permute-done.3.refs_3_ = bf16[48,3584]{1,0:T(8,128)(2,1)S(1)} collective-permute-done((bf16[48,3584]{1,0:T(8,128)(2,1)S(1)}, bf16[48,3584]{1,0:T(8,128)(2,1)S(1)}, u32[]{:S(2)}, u32[]{:S(2)}) %collective-permute-start.3) | collective-permute-done | bytes 344096 | tf_op jit(solution)/shard_map/ppermute | solution.py:253
  102.0 0.0 collective-permute-done.5.refs_5_
  102.0 1.0 choose.1
  103.0 0.0 copy-start.7
  103.0 0.8 copy-done.7
  103.8 2.4 %collective-permute-start.9 = (bf16[192,4096]{1,0:T(8,128)(2,1)S(1)}, bf16[192,4096]{1,0:T(8,128)(2,1)S(1)}, u32[]{:S(2)}, u32[]{:S(2)}) collective-permute-start(bf16[192,4096]{1,0:T(8,128)(2,1)S(1)} %get-tuple-element.33), channel_id=1, source_target_pairs={{0,8},{8,0},{1,9},{9,1},{2,10},{10,2},{3,11},{11,3},{4,12},{12,4},... | collective-permute-start | bytes 4718600 | tf_op jit(solution)/shard_map/ppermute | solution.py:265
  106.2 3.0 %collective-permute-done.9.oth = bf16[192,4096]{1,0:T(8,128)(2,1)S(1)} collective-permute-done((bf16[192,4096]{1,0:T(8,128)(2,1)S(1)}, bf16[192,4096]{1,0:T(8,128)(2,1)S(1)}, u32[]{:S(2)}, u32[]{:S(2)}) %collective-permute-start.9) | collective-permute-done | bytes 1572896 | tf_op jit(solution)/shard_map/ppermute | solution.py:265
  109.2 0.2 all-gather.2.cloned.1.call-done
  109.4 0.7 copy-done.18
  110.1 6.6 %forward.1 = (f32[384,1024]{1,0:T(8,128)S(1)}, bf16[384,1024]{1,0:T(8,128)(2,1)S(1)}) custom-call(s32[5]{0:T(128)S(1)} %copy-done.18, bf16[192,4096]{1,0:T(8,128)(2,1)S(1)} %get-tuple-element.30.own, bf16[192,4096]{1,0:T(8,128)(2,1)S(1)} %collective-permute-done.9.oth, bf16[8,1024,512]{2,1,0:T(8,128)(2,1)} %bitcast.10), custom_call_target="tpu_custom_call" | custom-call | flops 3221225472 | bytes 13631488 | tf_op jit(solution)/shard_map/forward/pallas_call | solution.py:268
  116.7 2.4 %collective-permute-start.10 = (bf16[384,1024]{1,0:T(8,128)(2,1)S(1)}, bf16[384,1024]{1,0:T(8,128)(2,1)S(1)}, u32[]{:S(2)}, u32[]{:S(2)}) collective-permute-start(bf16[384,1024]{1,0:T(8,128)(2,1)S(1)} %get-tuple-element.36), channel_id=1, source_target_pairs={{8,0},{10,2},{12,4},{14,6},{24,16},{26,18},{28,20},{30,22},{40,32}... | collective-permute-start | bytes 2359304 | tf_op jit(solution)/shard_map/ppermute | solution.py:277
  119.0 1.7 collective-permute-done.10.teach
  120.7 8.4 %backward.1 = (bf16[192,3584]{1,0:T(8,128)(2,1)S(1)}, bf16[192,3584]{1,0:T(8,128)(2,1)S(1)}, f32[1,3584]{1,0:T(1,128)S(1)}) custom-call(s32[5]{0:T(128)S(1)} %copy-done.18, f32[384,1024]{1,0:T(8,128)S(1)} %get-tuple-element.35.pred, bf16[384,1024]{1,0:T(8,128)(2,1)S(1)} %collective-permute-done.10.teach, bf16[192,1024]{1,0:T(8,128)(2,1)S(1)} %get-tuple-element.32.res_own, ...), custom_call_target="tpu_custom_call" | custom-call | flops 2818572288 | bytes 16777216 | tf_op jit(solution)/shard_map/backward/pallas_call | solution.py:278
  129.1 1.3 collective-permute-start.12
  130.4 1.3 collective-permute-start.11
  131.7 2.8 %collective-permute-done.11 = f32[28,128]{1,0:T(8,128)S(1)} collective-permute-done((f32[28,128]{1,0:T(8,128)S(1)}, f32[28,128]{1,0:T(8,128)S(1)}, u32[]{:S(2)}, u32[]{:S(2)}) %collective-permute-start.11) | collective-permute-done | bytes 14368 | tf_op jit(solution)/shard_map/ppermute | solution.py:289
  134.6 0.1 broadcast_in_dim.4
  134.7 2.6 %broadcast_select_fusion = bf16[192,3584]{1,0:T(8,128)(2,1)} fusion(bf16[192,3584]{1,0:T(8,128)(2,1)S(1)} %get-tuple-element.41, bf16[192,3584]{1,0:T(8,128)(2,1)} %collective-permute-done.12, pred[]{:T(512)S(6)} %eq.3), kind=kLoop, calls=%fused_computation | loop fusion | flops 688128 | bytes 4128769 | tf_op jit(solution)/shard_map/jit(_where)/select_n | solution.py:294
  137.3 0.0 reduce-scatter.2.cloned.1.call-update
  137.3 22.5 %all_to_all.15 = f32[32,28,128]{2,1,0:T(8,128)S(1)} all-to-all(f32[32,28,128]{2,1,0:T(8,128)S(1)} %broadcast_in_dim.4), channel_id=1, replica_groups={{0,64,128,192,256,320,384,448,2,66,130,194,258,322,386,450,4,68,132,196..., dimensions={0} | all-to-all | bytes 917504 | tf_op jit(solution)/shard_map/all_to_all | solution.py:292
  159.8 0.7 broadcast_in_dim.5
  160.5 10.5 %all-to-all-start.2 = ((f32[8,28,128]{2,1,0:T(8,128)}), f32[8,28,128]{2,1,0:T(8,128)S(1)}, u32[]{:S(2)}, u32[]{:S(2)}) async-start(f32[8,28,128]{2,1,0:T(8,128)} %broadcast_in_dim.5), calls=%async_computation.2 | async-start | bytes 262144 | tf_op jit(solution)/shard_map/all_to_all | solution.py:211
  171.0 0.0 reduce-scatter.2.cloned.1.call-done.summed
  171.0 1.0 copy-done.13
  172.0 2.4 %finish.1 = bf16[128,3584]{1,0:T(8,128)(2,1)} custom-call(s32[5]{0:T(128)S(1)} %copy-done.19, s32[1,384]{1,0:T(1,128)S(1)} %reshape.28.idx, bf16[48,3584]{1,0:T(8,128)(2,1)S(1)} %copy-done.13, bf16[48,3584]{1,0:T(8,128)(2,1)S(1)} %copy-done.12, f32[1,3584]{1,0:T(1,128)S(1)} %reshape.25.gain.gain_ref), custom_call_target="tpu_custom_call" | custom-call | flops 44040192 | bytes 4194304 | tf_op jit(solution)/shard_map/finish/pallas_call | solution.py:295
  174.5 5.1 %all-to-all-done.2 = f32[8,28,128]{2,1,0:T(8,128)S(1)} async-done(((f32[8,28,128]{2,1,0:T(8,128)}), f32[8,28,128]{2,1,0:T(8,128)S(1)}, u32[]{:S(2)}, u32[]{:S(2)}) %all-to-all-start.2) | async-done | bytes 114720 | tf_op jit(solution)/shard_map/all_to_all | solution.py:211
  179.6 0.6 multiply_reduce_fusion
  180.9 0.6 multiply_bitcast_fusion
  (46 shorter events, 0.2 us)
Async XLA Ops:
  8.0 9.7 %collective-permute-start = (bf16[64,512]{1,0:T(8,128)(2,1)S(1)}, bf16[64,512]{1,0:T(8,128)(2,1)S(1)}, u32[]{:S(2)}, u32[]{:S(2)}) collective-permute-start(bf16[64,512]{1,0:T(8,128)(2,1)S(1)} %pad_select_fusion), channel_id=1, source_target_pairs={{0,8},{8,0},{1,9},{9,1},{2,10},{10,2},{3,11},{11,3},{4,12},{12,4},... | collective-permute-start | bytes 196616 | tf_op jit(solution)/shard_map/ppermute | solution.py:237
  16.9 25.8 %copy-start.16 = (s32[5]{0:T(128)}, s32[5]{0:T(128)S(1)}, u32[]{:S(2)}) copy-start(s32[5]{0:T(128)S(1)} %stack.23.meta) | copy-start | bytes 64
  17.7 0.8 copy-start.14
  18.6 0.8 copy-start.15
  19.4 5.4 %copy-start.22 = (f32[3584]{0:T(1024)S(1)}, f32[3584]{0:T(1024)}, u32[]{:S(2)}) copy-start(f32[3584]{0:T(1024)} %param.12) | copy-start | bytes 43012
  19.4 5.4 %copy-start.23 = (s32[384]{0:T(512)S(1)}, s32[384]{0:T(512)}, u32[]{:S(2)}) copy-start(s32[384]{0:T(512)} %param.13) | copy-start | bytes 4612
  21.0 7.7 %copy-start.2 = (bf16[1024,512]{1,0:T(8,128)(2,1)S(1)}, bf16[1024,512]{1,0:T(8,128)(2,1)}, u32[]{:S(2)}) copy-start(bf16[1024,512]{1,0:T(8,128)(2,1)} %context.1) | copy-start | bytes 3145732
  21.0 7.7 %copy-start.3 = (bf16[1024,512]{1,0:T(8,128)(2,1)S(1)}, bf16[1024,512]{1,0:T(8,128)(2,1)}, u32[]{:S(2)}) copy-start(bf16[1024,512]{1,0:T(8,128)(2,1)} %residual.1) | copy-start | bytes 3145732
  21.0 21.7 %all-to-all-start = ((bf16[8,2,64,512]{3,2,1,0:T(8,128)(2,1)}), bf16[8,2,64,512]{3,2,1,0:T(8,128)(2,1)S(1)}, u32[]{:S(2)}, u32[]{:S(2)}) async-start(bf16[8,2,64,512]{3,2,1,0:T(8,128)(2,1)} %pair.1), calls=%async_computation | async-start | bytes 2097152 | tf_op jit(solution)/shard_map/all_to_all | solution.py:241
  24.7 84.7 %all-gather.2.cloned.1.call-start = ((), (), s32[]{:S(2)}) async-start(), calls=%async_computation.4 | async-start | bytes 9437184 | tf_op jit(solution)/shard_map/all_gather | solution.py:248
  25.0 1.2 copy-start.4
  27.2 0.7 copy-start.9
  27.9 0.8 copy-start.11
  32.0 0.7 copy-start.5
  32.7 0.8 copy-start.20
  33.5 19.3 %copy-start.10 = (bf16[48,3584]{1,0:T(8,128)(2,1)S(1)}, bf16[48,3584]{1,0:T(8,128)(2,1)}, u32[]{:S(2)}) copy-start(bf16[48,3584]{1,0:T(8,128)(2,1)} %copy-done.9) | copy-start | bytes 1032196
  42.7 1.7 copy-start.21
  42.7 23.7 %copy-start.6 = (bf16[192,1024]{1,0:T(8,128)(2,1)S(1)}, bf16[192,1024]{1,0:T(8,128)(2,1)}, u32[]{:S(2)}) copy-start(bf16[192,1024]{1,0:T(8,128)(2,1)} %copy-done.5) | copy-start | bytes 1179652
  44.4 126.6 %reduce-scatter.2.cloned.1.call-start = ((), (), s32[]{:S(2)}) async-start(), calls=%async_computation.5 | async-start | bytes 1720320 | tf_op jit(solution)/shard_map/reduce_scatter | solution.py:294
  44.4 22.0 %collective-permute-start.4 = (bf16[192,1024]{1,0:T(8,128)(2,1)S(1)}, bf16[192,1024]{1,0:T(8,128)(2,1)S(1)}, u32[]{:S(2)}, u32[]{:S(2)}) collective-permute-start(bf16[192,1024]{1,0:T(8,128)(2,1)S(1)} %copy-done.21), channel_id=1, source_target_pairs={{0,1},{1,0},{2,3},{3,2},{4,5},{5,4},{6,7},{7,6},{8,9},{9,8},{10,11... | collective-permute-start | bytes 1179656 | tf_op jit(solution)/shard_map/ppermute | solution.py:250
  52.8 24.0 %collective-permute-start.1 = (bf16[48,3584]{1,0:T(8,128)(2,1)S(1)}, bf16[48,3584]{1,0:T(8,128)(2,1)S(1)}, u32[]{:S(2)}, u32[]{:S(2)}) collective-permute-start(bf16[48,3584]{1,0:T(8,128)(2,1)S(1)} %copy-done.10), channel_id=1, source_target_pairs={{0,6},{2,0},{4,2},{6,4},{1,7},{3,1},{5,3},{7,5},{8,14},{10,8},{12,... | collective-permute-start | bytes 1032200 | tf_op jit(solution)/shard_map/ppermute | solution.py:253
  57.2 24.4 %collective-permute-start.2 = (bf16[48,3584]{1,0:T(8,128)(2,1)S(1)}, bf16[48,3584]{1,0:T(8,128)(2,1)S(1)}, u32[]{:S(2)}, u32[]{:S(2)}) collective-permute-start(bf16[48,3584]{1,0:T(8,128)(2,1)S(1)} %copy-done.10), channel_id=1, source_target_pairs={{0,4},{2,6},{4,0},{6,2},{1,5},{3,7},{5,1},{7,3},{8,12},{10,14},{12... | collective-permute-start | bytes 1032200 | tf_op jit(solution)/shard_map/ppermute | solution.py:253
  66.5 0.7 copy-start.17
  67.7 34.3 %collective-permute-start.5 = (bf16[192,1024]{1,0:T(8,128)(2,1)S(1)}, bf16[192,1024]{1,0:T(8,128)(2,1)S(1)}, u32[]{:S(2)}, u32[]{:S(2)}) collective-permute-start(bf16[192,1024]{1,0:T(8,128)(2,1)S(1)} %get-tuple-element.29.refs_4_), channel_id=1, source_target_pairs={{0,6},{2,0},{4,2},{6,4},{1,7},{3,1},{5,3},{7,5},{8,14},{10,8},{12,... | collective-permute-start | bytes 1179656 | tf_op jit(solution)/shard_map/ppermute | solution.py:253
  71.8 30.2 %collective-permute-start.6 = (bf16[192,1024]{1,0:T(8,128)(2,1)S(1)}, bf16[192,1024]{1,0:T(8,128)(2,1)S(1)}, u32[]{:S(2)}, u32[]{:S(2)}) collective-permute-start(bf16[192,1024]{1,0:T(8,128)(2,1)S(1)} %get-tuple-element.29.refs_4_), channel_id=1, source_target_pairs={{0,4},{2,6},{4,0},{6,2},{1,5},{3,7},{5,1},{7,3},{8,12},{10,14},{12... | collective-permute-start | bytes 1179656 | tf_op jit(solution)/shard_map/ppermute | solution.py:253
  74.2 27.8 %collective-permute-start.7 = (bf16[192,1024]{1,0:T(8,128)(2,1)S(1)}, bf16[192,1024]{1,0:T(8,128)(2,1)S(1)}, u32[]{:S(2)}, u32[]{:S(2)}) collective-permute-start(bf16[192,1024]{1,0:T(8,128)(2,1)S(1)} %get-tuple-element.29.refs_4_), channel_id=1, source_target_pairs={{0,2},{2,4},{4,6},{6,0},{1,3},{3,5},{5,7},{7,1},{8,10},{10,12},{12... | collective-permute-start | bytes 1179656 | tf_op jit(solution)/shard_map/ppermute | solution.py:253
  76.7 26.3 %collective-permute-start.8 = (bf16[192,1024]{1,0:T(8,128)(2,1)S(1)}, bf16[192,1024]{1,0:T(8,128)(2,1)S(1)}, u32[]{:S(2)}, u32[]{:S(2)}) collective-permute-start(bf16[192,1024]{1,0:T(8,128)(2,1)S(1)} %get-tuple-element.32.res_own), channel_id=1, source_target_pairs={{8,0},{10,2},{12,4},{14,6},{24,16},{26,18},{28,20},{30,22},{40,32}... | collective-permute-start | bytes 1179656 | tf_op jit(solution)/shard_map/ppermute | solution.py:259
  81.6 20.4 %collective-permute-start.3 = (bf16[48,3584]{1,0:T(8,128)(2,1)S(1)}, bf16[48,3584]{1,0:T(8,128)(2,1)S(1)}, u32[]{:S(2)}, u32[]{:S(2)}) collective-permute-start(bf16[48,3584]{1,0:T(8,128)(2,1)S(1)} %copy-done.10), channel_id=1, source_target_pairs={{0,2},{2,4},{4,6},{6,0},{1,3},{3,5},{5,7},{7,1},{8,10},{10,12},{12... | collective-permute-start | bytes 1032200 | tf_op jit(solution)/shard_map/ppermute | solution.py:253
  103.0 13.7 %copy-start = (bf16[192,4096]{1,0:T(8,128)(2,1)}, bf16[192,4096]{1,0:T(8,128)(2,1)S(1)}, u32[]{:S(2)}) copy-start(bf16[192,4096]{1,0:T(8,128)(2,1)S(1)} %get-tuple-element.30.own) | copy-start | bytes 4718596
  103.0 0.8 copy-start.7
  103.8 5.4 %collective-permute-start.9 = (bf16[192,4096]{1,0:T(8,128)(2,1)S(1)}, bf16[192,4096]{1,0:T(8,128)(2,1)S(1)}, u32[]{:S(2)}, u32[]{:S(2)}) collective-permute-start(bf16[192,4096]{1,0:T(8,128)(2,1)S(1)} %get-tuple-element.33), channel_id=1, source_target_pairs={{0,8},{8,0},{1,9},{9,1},{2,10},{10,2},{3,11},{11,3},{4,12},{12,4},... | collective-permute-start | bytes 4718600 | tf_op jit(solution)/shard_map/ppermute | solution.py:265
  109.2 7.4 %copy-start.1 = (bf16[192,4096]{1,0:T(8,128)(2,1)}, bf16[192,4096]{1,0:T(8,128)(2,1)S(1)}, u32[]{:S(2)}) copy-start(bf16[192,4096]{1,0:T(8,128)(2,1)S(1)} %collective-permute-done.9.oth) | copy-start | bytes 4718596
  109.4 0.7 copy-start.18
  110.1 10.6 %copy-start.8 = (bf16[192,1024]{1,0:T(8,128)(2,1)S(1)}, bf16[192,1024]{1,0:T(8,128)(2,1)}, u32[]{:S(2)}) copy-start(bf16[192,1024]{1,0:T(8,128)(2,1)} %copy-done.7) | copy-start | bytes 1179652
  116.7 4.0 %collective-permute-start.10 = (bf16[384,1024]{1,0:T(8,128)(2,1)S(1)}, bf16[384,1024]{1,0:T(8,128)(2,1)S(1)}, u32[]{:S(2)}, u32[]{:S(2)}) collective-permute-start(bf16[384,1024]{1,0:T(8,128)(2,1)S(1)} %get-tuple-element.36), channel_id=1, source_target_pairs={{8,0},{10,2},{12,4},{14,6},{24,16},{26,18},{28,20},{30,22},{40,32}... | collective-permute-start | bytes 2359304 | tf_op jit(solution)/shard_map/ppermute | solution.py:277
  129.1 5.5 %collective-permute-start.12 = (bf16[192,3584]{1,0:T(8,128)(2,1)S(1)}, bf16[192,3584]{1,0:T(8,128)(2,1)}, u32[]{:S(2)}, u32[]{:S(2)}) collective-permute-start(bf16[192,3584]{1,0:T(8,128)(2,1)S(1)} %get-tuple-element.39), channel_id=1, source_target_pairs={{0,8},{2,10},{4,12},{6,14},{16,24},{18,26},{20,28},{22,30},{32,40}... | collective-permute-start | bytes 4128776 | tf_op jit(solution)/shard_map/ppermute | solution.py:291
  130.4 4.1 %collective-permute-start.11 = (f32[28,128]{1,0:T(8,128)S(1)}, f32[28,128]{1,0:T(8,128)S(1)}, u32[]{:S(2)}, u32[]{:S(2)}) collective-permute-start(f32[28,128]{1,0:T(8,128)S(1)} %bitcast.12), channel_id=1, source_target_pairs={{0,8},{2,10},{4,12},{6,14},{16,24},{18,26},{20,28},{22,30},{32,40}... | collective-permute-start | bytes 43016 | tf_op jit(solution)/shard_map/ppermute | solution.py:289
  137.3 33.7 %copy-start.24 = (s32[384]{0:T(512)S(1)}, s32[384]{0:T(512)}, u32[]{:S(2)}) copy-start(s32[384]{0:T(512)} %param.13) | copy-start | bytes 4612
  137.3 33.7 %copy-start.12 = (bf16[48,3584]{1,0:T(8,128)(2,1)S(1)}, bf16[48,3584]{1,0:T(8,128)(2,1)}, u32[]{:S(2)}) copy-start(bf16[48,3584]{1,0:T(8,128)(2,1)} %copy-done.11) | copy-start | bytes 1032196
  137.3 33.8 %copy-start.19 = (s32[5]{0:T(128)S(1)}, s32[5]{0:T(128)}, u32[]{:S(2)}) copy-start(s32[5]{0:T(128)} %copy-done.16) | copy-start | bytes 64
  160.5 19.1 %all-to-all-start.2 = ((f32[8,28,128]{2,1,0:T(8,128)}), f32[8,28,128]{2,1,0:T(8,128)S(1)}, u32[]{:S(2)}, u32[]{:S(2)}) async-start(f32[8,28,128]{2,1,0:T(8,128)} %broadcast_in_dim.5), calls=%async_computation.2 | async-start | bytes 262144 | tf_op jit(solution)/shard_map/all_to_all | solution.py:211
  171.0 1.0 copy-start.13
Sparse Core Ops, SparseCore 0:
  44.5 64.8 all-gather.1
  137.4 31.2 reduce-scatter.1
